TPU v7x, 32 devices: a whole 2x2x4 slice. The times are simulated.
32 devices in a mesh: dp: 8 (over y, x, core), tensor: 4 (over z).
Axes of the slice: x: 2, y: 2, z: 4, core: 2. Of those that a mesh axis runs over, the one named last changes fastest.
Arguments:
- tokens: bfloat16 [16384, 1024], P(('dp', 'tensor')), may hold values from -6 to 6
- w_qkv: bfloat16 [1024, 3, 1024], P('dp', None, 'tensor'), may hold values from -0.25 to 0.25
- w_out: bfloat16 [1024, 1024], P('tensor', 'dp'), may hold values from -0.5 to 0.5
- w_in: bfloat16 [1024, 2, 2624], P('dp', None, 'tensor'), may hold values from -0.1875 to 0.1875
- w_down: bfloat16 [2624, 1024], P('tensor', 'dp'), may hold values from -0.125 to 0.125
- gain_attn: bfloat16 [1024], P('dp'), may hold values from 0.5 to 1.5
- gain_mlp: bfloat16 [1024], P('dp'), may hold values from 0.5 to 1.5
- grad_output: bfloat16 [16384, 1024], P(('dp', 'tensor')), may hold values from -6 to 6
Outputs:
- output: bfloat16 [16384, 1024], P(('dp', 'tensor'))
- grad_tokens: bfloat16 [16384, 1024], P(('dp', 'tensor'))
- grad_qkv: float32 [1024, 3, 1024], P('dp', None, 'tensor')
- grad_out: float32 [1024, 1024], P('tensor', 'dp')
- grad_in: float32 [1024, 2, 2624], P('dp', None, 'tensor')
- grad_down: float32 [2624, 1024], P('tensor', 'dp')
- grad_gain_attn: float32 [1024], P('dp')
- grad_gain_mlp: float32 [1024], P('dp')
All inputs are finite; a program needn't handle non-finite values.
Results may differ from a plain program's by a relative error of at most 0.017.
The roundings to bfloat16 on the way count: a program that leaves them out, or rounds other values in their place, can miss the bound.
Values may be sent and summed in bfloat16 or wider, within the bound.
A program may use at most 192 MiB of HBM per device.

v0:
```python
import jax
import jax.numpy as jnp
from jax import lax
from jax.sharding import PartitionSpec as P

HD = 64
LEN = 1024


EPS = 1e-05
THETA = 160000.0


def layer_norm(values, gain):
    centred = values - jnp.mean(values, axis=-1, keepdims=True)
    spread = jnp.mean(centred * centred, axis=-1, keepdims=True)
    return centred * lax.rsqrt(spread + EPS) * gain


def rotary(values, length):
    rows = values.shape[0]
    half = values.shape[-1] // 2
    freq = THETA ** (-(jnp.arange(half).astype(jnp.float32) * 2.0 / values.shape[-1]))
    place = (jnp.arange(rows) % length).astype(jnp.float32)
    angle = place[:, None] * freq[None, :]
    cosine = jnp.cos(angle)[:, None, :]
    sine = jnp.sin(angle)[:, None, :]
    first = values[..., :half]
    second = values[..., half:]
    return jnp.concatenate(
        [first * cosine - second * sine, second * cosine + first * sine], axis=-1
    )


def geglu(pair):
    return jax.nn.gelu(pair[:, 0], approximate=False) * pair[:, 1]


def rotate_seq(values):
    return rotary(values, LEN)


def attend(query, key, value, length):
    rows, heads, size = query.shape
    block = min(512, length)
    scale = size ** (-0.5)

    def single(index):
        start = index * block
        first = start // length * length
        query_block = lax.dynamic_slice_in_dim(query, start, block, 0)
        key_seq = lax.dynamic_slice_in_dim(key, first, length, 0)
        value_seq = lax.dynamic_slice_in_dim(value, first, length, 0)
        scores = (
            jnp.einsum("qhe,khe->hqk", query_block, key_seq, preferred_element_type=jnp.float32)
            * scale
        )
        highest = jnp.max(scores, axis=-1, keepdims=True)
        total = jnp.sum(jnp.exp(scores - highest), axis=-1, keepdims=True)
        lse = highest + jnp.log(total)
        probs = jnp.exp(scores - lse).astype(jnp.bfloat16)
        result = jnp.einsum("hqk,khe->qhe", probs, value_seq, preferred_element_type=jnp.float32)
        return (result, lse[..., 0])

    results, lses = lax.map(single, jnp.arange(rows // block))
    return (results.reshape(rows, heads, size), lses)


def attend_back(query, key, value, lses, grad_att, length):
    rows, heads, size = query.shape
    block = min(512, length)
    scale = size ** (-0.5)
    zeros = jnp.zeros((rows, heads, size), jnp.float32)

    def step(index, carry):
        grad_query, grad_key, grad_value = carry
        start = index * block
        first = start // length * length
        query_block = lax.dynamic_slice_in_dim(query, start, block, 0)
        grad_block = lax.dynamic_slice_in_dim(grad_att, start, block, 0)
        key_seq = lax.dynamic_slice_in_dim(key, first, length, 0)
        value_seq = lax.dynamic_slice_in_dim(value, first, length, 0)
        lse = lax.dynamic_index_in_dim(lses, index, 0, keepdims=False)
        scores = (
            jnp.einsum("qhe,khe->hqk", query_block, key_seq, preferred_element_type=jnp.float32)
            * scale
        )
        probs = jnp.exp(scores - lse[..., None])
        dprob = jnp.einsum(
            "qhe,khe->hqk", grad_block, value_seq, preferred_element_type=jnp.float32
        )
        inner = jnp.sum(dprob * probs, axis=-1, keepdims=True)
        grad_scores = (probs * (dprob - inner)).astype(jnp.bfloat16)
        part_query = (
            jnp.einsum("hqk,khe->qhe", grad_scores, key_seq, preferred_element_type=jnp.float32)
            * scale
        )
        part_key = (
            jnp.einsum("hqk,qhe->khe", grad_scores, query_block, preferred_element_type=jnp.float32)
            * scale
        )
        part_value = jnp.einsum(
            "hqk,qhe->khe",
            probs.astype(jnp.bfloat16),
            grad_block,
            preferred_element_type=jnp.float32,
        )
        grad_query = lax.dynamic_update_slice_in_dim(grad_query, part_query, start, 0)
        grad_key = lax.dynamic_update_slice_in_dim(
            grad_key, lax.dynamic_slice_in_dim(grad_key, first, length, 0) + part_key, first, 0
        )
        grad_value = lax.dynamic_update_slice_in_dim(
            grad_value,
            lax.dynamic_slice_in_dim(grad_value, first, length, 0) + part_value,
            first,
            0,
        )
        return (grad_query, grad_key, grad_value)

    return lax.fori_loop(0, rows // block, step, (zeros, zeros, zeros))


def local(tokens, w_qkv, w_out, w_in, w_down, gain_attn, gain_mlp, grad_output):
    gathered_w = (
        lax.all_gather(w_qkv, "dp", axis=0, tiled=True),
        lax.all_gather(w_out, "dp", axis=1, tiled=True),
        lax.all_gather(w_in, "dp", axis=0, tiled=True),
        lax.all_gather(w_down, "dp", axis=1, tiled=True),
        lax.all_gather(gain_attn, "dp", axis=0, tiled=True),
        lax.all_gather(gain_mlp, "dp", axis=0, tiled=True),
    )
    qkv_w, out_w, in_w, down_w, gain_first, gain_second = gathered_w
    gain_one = gain_first.astype(jnp.float32)
    gain_two = gain_second.astype(jnp.float32)
    inputs = tokens.astype(jnp.float32)
    normed_one = layer_norm(inputs, gain_one).astype(jnp.bfloat16)
    gathered_one = lax.all_gather(normed_one, "tensor", axis=0, tiled=True)
    rows = gathered_one.shape[0]
    heads = qkv_w.shape[2] // HD
    projected = jnp.einsum("td,dcf->tcf", gathered_one, qkv_w, preferred_element_type=jnp.float32)
    split = projected.reshape(rows, 3, heads, HD)
    query_f = split[:, 0]
    query_b = rotary(query_f, LEN).astype(jnp.bfloat16)
    key_b = rotary(split[:, 1], LEN).astype(jnp.bfloat16)
    value_b = split[:, 2].astype(jnp.bfloat16)
    attended, lses = attend(query_b, key_b, value_b, LEN)
    attended_b = attended.reshape(rows, heads * HD).astype(jnp.bfloat16)
    branch_one = lax.psum_scatter(
        jnp.dot(attended_b, out_w, preferred_element_type=jnp.float32),
        "tensor",
        scatter_dimension=0,
        tiled=True,
    )
    residual = inputs + branch_one
    normed_two = layer_norm(residual, gain_two).astype(jnp.bfloat16)
    gathered_two = lax.all_gather(normed_two, "tensor", axis=0, tiled=True)
    pair = jnp.einsum("td,dcf->tcf", gathered_two, in_w, preferred_element_type=jnp.float32)
    hidden = geglu(pair).astype(jnp.bfloat16)
    branch_two = lax.psum_scatter(
        jnp.dot(hidden, down_w, preferred_element_type=jnp.float32).astype(jnp.bfloat16),
        "tensor",
        scatter_dimension=0,
        tiled=True,
    ).astype(jnp.float32)
    output = (residual + branch_two).astype(jnp.bfloat16)
    regathered = (
        lax.all_gather(w_qkv, "dp", axis=0, tiled=True),
        lax.all_gather(w_out, "dp", axis=1, tiled=True),
        lax.all_gather(w_in, "dp", axis=0, tiled=True),
        lax.all_gather(w_down, "dp", axis=1, tiled=True),
        lax.all_gather(gain_attn, "dp", axis=0, tiled=True),
        lax.all_gather(gain_mlp, "dp", axis=0, tiled=True),
    )
    qkv_w, out_w, in_w, down_w, gain_first, gain_second = regathered
    gain_one = gain_first.astype(jnp.float32)
    gain_two = gain_second.astype(jnp.float32)
    grad_top = grad_output.astype(jnp.float32)
    grad_all = lax.all_gather(grad_output, "tensor", axis=0, tiled=True)
    grad_down = jnp.einsum("tf,td->fd", hidden, grad_all, preferred_element_type=jnp.float32)
    grad_hidden = jnp.einsum("td,fd->tf", grad_all, down_w, preferred_element_type=jnp.float32)
    geglu_pull = jax.vjp(geglu, pair)[1]
    grad_pair = geglu_pull(grad_hidden)[0].astype(jnp.bfloat16)
    grad_in = jnp.einsum("td,tcf->dcf", gathered_two, grad_pair, preferred_element_type=jnp.float32)
    grad_normed_two = lax.psum_scatter(
        jnp.einsum("tcf,dcf->td", grad_pair, in_w, preferred_element_type=jnp.float32),
        "tensor",
        scatter_dimension=0,
        tiled=True,
    )
    norm_pull_two = jax.vjp(layer_norm, residual, gain_two)[1]
    grad_res_part, grad_gain_two = norm_pull_two(grad_normed_two)
    grad_residual = grad_top + grad_res_part
    grad_res_b = grad_residual.astype(jnp.bfloat16)
    grad_res_all = lax.all_gather(grad_res_b, "tensor", axis=0, tiled=True)
    grad_out_w = jnp.einsum(
        "tf,td->fd", attended_b, grad_res_all, preferred_element_type=jnp.float32
    )
    grad_att = jnp.einsum("td,fd->tf", grad_res_all, out_w, preferred_element_type=jnp.float32)
    grad_att = grad_att.astype(jnp.bfloat16).reshape(rows, heads, HD)
    grad_query, grad_key, grad_value = attend_back(query_b, key_b, value_b, lses, grad_att, LEN)
    rotary_pull = jax.vjp(rotate_seq, query_f)[1]
    back_query = rotary_pull(grad_query)[0]
    back_key = rotary_pull(grad_key)[0]
    grad_proj = (
        jnp.stack([back_query, back_key, grad_value], axis=1)
        .reshape(rows, 3, heads * HD)
        .astype(jnp.bfloat16)
    )
    grad_qkv_w = jnp.einsum(
        "td,tcf->dcf", gathered_one, grad_proj, preferred_element_type=jnp.float32
    )
    grad_normed_one = lax.psum_scatter(
        jnp.einsum("tcf,dcf->td", grad_proj, qkv_w, preferred_element_type=jnp.float32),
        "tensor",
        scatter_dimension=0,
        tiled=True,
    )
    norm_pull_one = jax.vjp(layer_norm, inputs, gain_one)[1]
    grad_in_part, grad_gain_one = norm_pull_one(grad_normed_one)
    grad_tokens = (grad_residual + grad_in_part).astype(jnp.bfloat16)
    summed = (
        lax.psum_scatter(grad_qkv_w, "dp", scatter_dimension=0, tiled=True),
        lax.psum_scatter(grad_out_w, "dp", scatter_dimension=1, tiled=True),
        lax.psum_scatter(grad_in, "dp", scatter_dimension=0, tiled=True),
        lax.psum_scatter(grad_down, "dp", scatter_dimension=1, tiled=True),
        lax.psum_scatter(grad_gain_one, "dp", scatter_dimension=0, tiled=True),
        lax.psum_scatter(grad_gain_two, "dp", scatter_dimension=0, tiled=True),
    )
    gain_first_grad, gain_second_grad = lax.psum((summed[4], summed[5]), "tensor")
    return (
        output,
        grad_tokens,
        summed[0],
        summed[1],
        summed[2],
        summed[3],
        gain_first_grad,
        gain_second_grad,
    )


def solution(mesh):
    placed = (
        P(("dp", "tensor"), None),
        P("dp", None, "tensor"),
        P("tensor", "dp"),
        P("dp", None, "tensor"),
        P("tensor", "dp"),
        P("dp"),
        P("dp"),
        P(("dp", "tensor"), None),
    )
    return jax.shard_map(
        local,
        mesh=mesh,
        in_specs=placed,
        out_specs=(
            P(("dp", "tensor"), None),
            P(("dp", "tensor"), None),
            P("dp", None, "tensor"),
            P("tensor", "dp"),
            P("dp", None, "tensor"),
            P("tensor", "dp"),
            P("dp"),
            P("dp"),
        ),
        check_vma=False,
    )
```

profile of v0, /device:TPU:0, one launch (start us, length us, event | category | flops | bytes accessed | tf_op | source)
XLA Modules:
  0.0 1317.4 jit_solution(13067545842820573546)
XLA Ops:
  9.0 10.3 all-gather
  26.4 12.3 all_gather.39
  40.5 82.9 %all-gather.10.cloned.1.call-done = bf16[2048,1024]{1,0:T(8,128)(2,1)} async-done(((bf16[512,1024]{1,0:T(8,128)(2,1)}), bf16[2048,1024]{1,0:T(8,128)(2,1)}) %all-gather.10.cloned.1.call-update) | async-done | bytes 4194320 | tf_op jit(solution)/shard_map/all_gather | solution.py:137
  123.4 5.7 fusion.70
  130.6 29.7 %while.33 = (s32[]{:T(128)}, bf16[4,512,4,64]{1,3,2,0:T(8,128)(2,1)}, f32[4,4,512]{2,1,0:T(4,128)S(1)}, s32[4]{0:T(128)S(1)}, bf16[2048,4,64]{0,2,1:T(8,128)(2,1...) while((s32[]{:T(128)}, ...), condition=%wide.region_5.6_spmd, body=%wide.region_2.5_spmd.sunk | while | flops 553646080 | bytes 35455444 | solution.py:65
  170.8 9.0 all-gather.1
  179.8 132.3 %reduce-scatter.9.cloned.1.call-done = f32[512,1024]{1,0:T(8,128)} async-done(((f32[2048,1024]{1,0:T(8,128)}), f32[512,1024]{1,0:T(8,128)}) %reduce-scatter.9.cloned.1.call-update) | async-done | bytes 2097168 | tf_op jit(solution)/shard_map/reduce_scatter | solution.py:148
  316.0 23.5 %all-gather.18.cloned.1.call-done = bf16[656,1024]{1,0:T(8,128)(2,1)} async-done(((bf16[656,128]{1,0:T(8,128)(2,1)}), bf16[656,1024]{1,0:T(8,128)(2,1)}) %all-gather.18.cloned.1.call-update) | async-done | bytes 1343504 | tf_op jit(solution)/shard_map/all_gather | solution.py:128
  339.5 82.2 %all-gather.20.cloned.1.call-done = bf16[2048,1024]{1,0:T(8,128)(2,1)} async-done(((bf16[512,1024]{1,0:T(8,128)(2,1)}), bf16[2048,1024]{1,0:T(8,128)(2,1)}) %all-gather.20.cloned.1.call-update) | async-done | bytes 4194320 | tf_op jit(solution)/shard_map/all_gather | solution.py:178
  421.7 7.9 fusion.99
  429.7 23.2 %all-gather.16.cloned.1.call-done = bf16[1024,2,656]{0,2,1:T(8,128)(2,1)} async-done(((bf16[128,2,656]{0,2,1:T(8,128)(2,1)}), bf16[1024,2,656]{0,2,1:T(8,128)(2,1)}) %all-gather.16.cloned.1.call-update) | async-done | bytes 2686992 | tf_op jit(solution)/shard_map/all_gather | solution.py:127
  452.8 82.9 %all-gather.14.cloned.1.call-done = bf16[2048,1024]{1,0:T(8,128)(2,1)} async-done(((bf16[512,1024]{1,0:T(8,128)(2,1)}), bf16[2048,1024]{1,0:T(8,128)(2,1)}) %all-gather.14.cloned.1.call-update) | async-done | bytes 4194320 | tf_op jit(solution)/shard_map/all_gather | solution.py:156
  535.8 8.5 fusion.66
  544.3 12.5 multiply_bitcast_fusion
  562.0 13.5 %convolution_bitcast_fusion.1 = f32[2048,1024]{1,0:T(8,128)} fusion(bf16[1024,2,656]{0,2,1:T(8,128)(2,1)} %all-gather.16.cloned.1.call-done, f32[2048,1,656]{0,2,1:T(8,128)} %get-tuple-element.379, f32[2048,1,656]{0,2,1:T(8,128)} %get-tuple-element.371), kind=kOutput, calls=%fused_computation.82 | convolution fusion | flops 5508300800 | bytes 21823488 | tf_op jit(solution)/shard_map/tcf,dcf->td/dot_general | solution.py:185
  575.6 11.9 reduce-scatter.11.cloned.1.call-start
  587.5 7.7 convolution_convert_fusion
  595.2 123.5 %reduce-scatter.13.cloned.1.call-done = f32[512,1024]{1,0:T(8,128)} async-done(((f32[2048,1024]{1,0:T(8,128)}), f32[512,1024]{1,0:T(8,128)}) %reduce-scatter.13.cloned.1.call-update) | async-done | bytes 2097168 | tf_op jit(solution)/shard_map/reduce_scatter | solution.py:184
  721.6 77.0 %reduce-scatter.11.cloned.1.call-done = bf16[512,1024]{1,0:T(8,128)(2,1)} async-done(((bf16[2048,1024]{1,0:T(8,128)(2,1)}), bf16[512,1024]{1,0:T(8,128)(2,1)}) %reduce-scatter.11.cloned.1.call-update) | async-done | bytes 1048592 | tf_op jit(solution)/shard_map/reduce_scatter | solution.py:159
  805.0 81.4 %all-gather.22.cloned.1.call-done = bf16[2048,1024]{1,0:T(8,128)(2,1)} async-done(((bf16[512,1024]{1,0:T(8,128)(2,1)}), bf16[2048,1024]{1,0:T(8,128)(2,1)}) %all-gather.22.cloned.1.call-update) | async-done | bytes 4194320 | tf_op jit(solution)/shard_map/all_gather | solution.py:194
  894.2 53.7 %while.34 = (s32[]{:T(128)}, f32[2048,4,64]{0,2,1:T(8,128)}, f32[2048,4,64]{0,2,1:T(8,128)S(1)}, f32[2048,4,64]{0,2,1:T(8,128)}, bf16[2048,4,64]{0,2,1:T(8,128)(...) while((s32[]{:T(128)}, f32[2048,4,64]{0,2,1:T(8,128)}, ...), condition=%wide.region_15.16_spmd, body=%wide.region_13.15_spmd.sunk | while | flops 1368258560 | bytes 95478312 | solution.py:120
  956.5 9.1 convolution_bitcast_fusion
  967.3 6.6 fusion.101
  974.0 11.2 fusion.64
  991.0 7.7 fusion.68
  1000.1 108.7 %reduce-scatter.15.cloned.1.call-done = f32[512,1024]{1,0:T(8,128)} async-done(((f32[2048,1024]{1,0:T(8,128)}), f32[512,1024]{1,0:T(8,128)}) %reduce-scatter.15.cloned.1.call-update) | async-done | bytes 2097168 | tf_op jit(solution)/shard_map/reduce_scatter | solution.py:212
  1112.1 13.7 %all-reduce.8 = (f32[1024]{0:T(1024)S(1)}, f32[1024]{0:T(1024)S(1)}) all-reduce(f32[1024]{0:T(1024)S(1)} %get-tuple-element.329, f32[1024]{0:T(1024)S(1)} %copy-done.37), channel_id=10, replica_groups=mesh['dp'=8,'tensor'=4] {'dp'}, use_global_device_ids=true, to_apply=%region_24.25.clone | all-reduce | flops 2048 | bytes 16384
  1125.9 12.1 all-reduce.9
  1141.3 17.2 %reduce-scatter.23.cloned.1.call-done = f32[656,128]{1,0:T(8,128)} async-done(((f32[656,1024]{1,0:T(8,128)}), f32[656,128]{1,0:T(8,128)}) %reduce-scatter.23.cloned.1.call-update) | async-done | bytes 335888 | tf_op jit(solution)/shard_map/reduce_scatter | solution.py:225
  1158.5 61.6 %reduce-scatter.21.cloned.1.call-done = f32[128,2,656]{0,2,1:T(8,128)} async-done(((f32[1024,2,656]{0,2,1:T(8,128)}), f32[128,2,656]{0,2,1:T(8,128)}) %reduce-scatter.21.cloned.1.call-update) | async-done | bytes 671760 | tf_op jit(solution)/shard_map/reduce_scatter | solution.py:224
  1220.1 40.0 %reduce-scatter.19.cloned.1.call-done = f32[256,128]{1,0:T(8,128)} async-done(((f32[256,1024]{1,0:T(8,128)}), f32[256,128]{1,0:T(8,128)}) %reduce-scatter.19.cloned.1.call-update) | async-done | bytes 131088 | tf_op jit(solution)/shard_map/reduce_scatter | solution.py:223
  1260.1 50.5 %reduce-scatter.17.cloned.1.call-done = f32[128,3,256]{2,0,1:T(8,128)} async-done(((f32[1024,3,256]{2,0,1:T(8,128)}), f32[128,3,256]{2,0,1:T(8,128)}) %reduce-scatter.17.cloned.1.call-update) | async-done | bytes 393232 | tf_op jit(solution)/shard_map/reduce_scatter | solution.py:222
  (246 shorter events, 152.1 us)
Async XLA Ops:
  7.2 19.2 %copy-start.30 = (bf16[256,128]{1,0:T(8,128)(2,1)S(1)}, bf16[256,128]{1,0:T(8,128)(2,1)}, u32[]{:S(2)}) copy-start(bf16[256,128]{1,0:T(8,128)(2,1)} %param.14) | copy-start | bytes 196612
  7.2 33.4 %all-gather.12.cloned.1.call-start = ((), (), s32[]{:S(2)}) async-start(), calls=%async_computation.9 | async-start | bytes 1769472 | tf_op jit(solution)/shard_map/all_gather | solution.py:125
  9.0 114.4 %all-gather.10.cloned.1.call-start = ((), (), s32[]{:S(2)}) async-start(), calls=%async_computation.8 | async-start | bytes 5242880 | tf_op jit(solution)/shard_map/all_gather | solution.py:137
  26.3 285.9 %reduce-scatter.9.cloned.1.call-start = ((), (), s32[]{:S(2)}) async-start(), calls=%async_computation.10 | async-start | bytes 10485760 | tf_op jit(solution)/shard_map/reduce_scatter | solution.py:148
  39.7 90.1 %copy-start.16 = (f32[2048,32]{0,1:T(8,128)}, f32[2048,32]{0,1:T(8,128)S(1)}, u32[]{:S(2)}) copy-start(f32[2048,32]{0,1:T(8,128)S(1)} %get-tuple-element.396) | copy-start | bytes 786436
  39.7 90.1 %copy-start.18 = (f32[2048,32]{0,1:T(8,128)}, f32[2048,32]{0,1:T(8,128)S(1)}, u32[]{:S(2)}) copy-start(f32[2048,32]{0,1:T(8,128)S(1)} %get-tuple-element.397) | copy-start | bytes 786436
  160.4 8.6 copy-start.3
  160.4 8.6 copy-start.5
  169.0 170.5 %all-gather.18.cloned.1.call-start = ((), (), s32[]{:S(2)}) async-start(), calls=%async_computation.13 | async-start | bytes 1511424 | tf_op jit(solution)/shard_map/all_gather | solution.py:128
  169.6 252.1 %all-gather.20.cloned.1.call-start = ((), (), s32[]{:S(2)}) async-start(), calls=%async_computation.15 | async-start | bytes 5242880 | tf_op jit(solution)/shard_map/all_gather | solution.py:178
  170.2 282.6 %all-gather.16.cloned.1.call-start = ((), (), s32[]{:S(2)}) async-start(), calls=%async_computation.12 | async-start | bytes 3022848 | tf_op jit(solution)/shard_map/all_gather | solution.py:127
  170.8 365.0 %all-gather.14.cloned.1.call-start = ((), (), s32[]{:S(2)}) async-start(), calls=%async_computation.11 | async-start | bytes 5242880 | tf_op jit(solution)/shard_map/all_gather | solution.py:156
  316.0 402.7 %reduce-scatter.13.cloned.1.call-start = ((), (), s32[]{:S(2)}) async-start(), calls=%async_computation.16 | async-start | bytes 10485760 | tf_op jit(solution)/shard_map/reduce_scatter | solution.py:184
  535.8 8.6 copy-start.6
  575.6 223.0 %reduce-scatter.11.cloned.1.call-start = ((), (), s32[]{:S(2)}) async-start(), calls=%async_computation.14 | async-start | bytes 5242880 | tf_op jit(solution)/shard_map/reduce_scatter | solution.py:159
  595.2 291.2 %all-gather.22.cloned.1.call-start = ((), (), s32[]{:S(2)}) async-start(), calls=%async_computation.17 | async-start | bytes 5242880 | tf_op jit(solution)/shard_map/all_gather | solution.py:194
  802.2 84.1 %copy-start.20 = (bf16[256,1024]{1,0:T(8,128)(2,1)S(1)}, bf16[256,1024]{1,0:T(8,128)(2,1)}, u32[]{:S(2)}) copy-start(bf16[256,1024]{1,0:T(8,128)(2,1)} %all_gather.39) | copy-start | bytes 1572868
  802.2 88.6 %copy-start.33 = (f32[512]{0:T(512)}, f32[512]{0:T(512)S(1)}, u32[]{:S(2)}) copy-start(f32[512]{0:T(512)S(1)} %negate_multiply_fusion.2) | copy-start | bytes 6148
  804.9 303.9 %reduce-scatter.15.cloned.1.call-start = ((), (), s32[]{:S(2)}) async-start(), calls=%async_computation.18 | async-start | bytes 10485760 | tf_op jit(solution)/shard_map/reduce_scatter | solution.py:212
  956.4 9.1 copy-start.23
  965.6 192.8 %reduce-scatter.23.cloned.1.call-start = ((), (), s32[]{:S(2)}) async-start(), calls=%async_computation.22 | async-start | bytes 3022848 | tf_op jit(solution)/shard_map/reduce_scatter | solution.py:225
  974.0 246.1 %reduce-scatter.21.cloned.1.call-start = ((), (), s32[]{:S(2)}) async-start(), calls=%async_computation.21 | async-start | bytes 6045696 | tf_op jit(solution)/shard_map/reduce_scatter | solution.py:224
  985.3 274.8 %reduce-scatter.19.cloned.1.call-start = ((), (), s32[]{:S(2)}) async-start(), calls=%async_computation.20 | async-start | bytes 1179648 | tf_op jit(solution)/shard_map/reduce_scatter | solution.py:223
  990.9 117.9 %copy-start = (bf16[512,1024]{1,0:T(8,128)(2,1)S(1)}, bf16[512,1024]{1,0:T(8,128)(2,1)}, u32[]{:S(2)}) copy-start(bf16[512,1024]{1,0:T(8,128)(2,1)} %param.12) | copy-start | bytes 3145732
  990.9 117.9 %copy-start.27 = (f32[8,1,128]{2,1,0:T(1,128)S(1)}, f32[8,1,128]{2,1,0:T(1,128)}, u32[]{:S(2)}) copy-start(f32[8,1,128]{2,1,0:T(1,128)} %copy-done.26) | copy-start | bytes 12292
  990.9 117.9 %copy-start.29 = (f32[512]{0:T(512)S(1)}, f32[512]{0:T(512)}, u32[]{:S(2)}) copy-start(f32[512]{0:T(512)} %copy-done.28) | copy-start | bytes 6148
  990.9 319.6 %reduce-scatter.17.cloned.1.call-start = ((), (), s32[]{:S(2)}) async-start(), calls=%async_computation.19 | async-start | bytes 3538944 | tf_op jit(solution)/shard_map/reduce_scatter | solution.py:222
  998.7 112.3 %copy-start.36 = (f32[512]{0:T(512)S(1)}, f32[512]{0:T(512)}, u32[]{:S(2)}) copy-start(f32[512]{0:T(512)} %copy-done.35) | copy-start | bytes 6148
  998.7 112.3 %copy-start.32 = (f32[512]{0:T(512)S(1)}, f32[512]{0:T(512)}, u32[]{:S(2)}) copy-start(f32[512]{0:T(512)} %copy-done.31) | copy-start | bytes 6148
  998.7 113.4 %copy-start.37 = (f32[1024]{0:T(1024)S(1)}, f32[1024]{0:T(1024)}, u32[]{:S(2)}) copy-start(f32[1024]{0:T(1024)} %get-tuple-element.327) | copy-start | bytes 12292
  998.7 139.3 %copy-start.8 = (f32[512,1024]{1,0:T(8,128)S(1)}, f32[512,1024]{1,0:T(8,128)}, u32[]{:S(2)}) copy-start(f32[512,1024]{1,0:T(8,128)} %copy-done.7) | copy-start | bytes 6291460
  998.7 139.3 %copy-start.34 = (f32[512]{0:T(512)S(1)}, f32[512]{0:T(512)}, u32[]{:S(2)}) copy-start(f32[512]{0:T(512)} %copy-done.33) | copy-start | bytes 6148
  (41 other events, 99.3 us)
Sparse Core Ops, SparseCore 0:
  10.5 30.0 all-gather.11
  42.7 80.7 all-gather.9
  169.1 142.9 reduce-scatter.8
  313.9 25.5 all-gather.17
  340.9 80.7 all-gather.19
  423.5 29.3 all-gather.15
  455.0 80.7 all-gather.13
  575.7 142.9 reduce-scatter.12
  721.0 77.4 reduce-scatter.10
  805.0 81.2 all-gather.21
  965.7 142.9 reduce-scatter.14
  1113.0 45.3 reduce-scatter.22
  1162.8 57.1 reduce-scatter.20
  1224.0 36.0 reduce-scatter.18
  1264.3 46.2 reduce-scatter.16
where the time goes:
time: 1330 us; the launch traced here: 1320 us
  waiting for transfers between devices  989 us (74%)
  matrix products  150 us (11%)
  other arithmetic  64.2 us (5%)
  blocking collectives  57.4 us (4%)
  local copies, waits for them, and re-layouts  25.2 us (2%)
  between operations  15.4 us (1%)
    reduce_scatter x1, waiting for transfers between devices, local(): lax.psum_scatter(jnp.dot(attended_b, out_w, preferred_element_type=jnp.fl...  132 us
    reduce_scatter x1, waiting for transfers between devices, local(): lax.psum_scatter(jnp.einsum('tcf,dcf->td', grad_pair, in_w, preferred_ele...  124 us
    reduce_scatter x1, waiting for transfers between devices, local(): lax.psum_scatter(jnp.einsum('tcf,dcf->td', grad_proj, qkv_w, preferred_el...  109 us
    all_gather x1, waiting for transfers between devices, local(): gathered_two = lax.all_gather(normed_two, 'tensor', axis=0, tiled=True)  82.9 us
    all_gather x1, waiting for transfers between devices, local(): gathered_one = lax.all_gather(normed_one, 'tensor', axis=0, tiled=True)  82.9 us
    all_gather x1, waiting for transfers between devices, local(): grad_all = lax.all_gather(grad_output, 'tensor', axis=0, tiled=True)  82.2 us
    all_gather x1, waiting for transfers between devices, local(): grad_res_all = lax.all_gather(grad_res_b, 'tensor', axis=0, tiled=True)  81.4 us
    reduce_scatter x1, waiting for transfers between devices, local(): lax.psum_scatter(jnp.dot(hidden, down_w, preferred_element_type=jnp.float...  77 us
  transfers between devices with their start and end apart: 15, of which 15 were waited for; matrix products, arithmetic and copies ran while one was open for 5% of the time, Pallas kernels for 0%

commit v1 on v0

v1 whole, which is shorter than its diff:
```python
import functools

import jax
import jax.numpy as jnp
from jax import lax
from jax.experimental import pallas as pl
from jax.experimental.pallas import tpu as pltpu
from jax.sharding import PartitionSpec as P

HD = 64
LEN = 1024
EPS = 1e-05
THETA = 160000.0
MESH = pl.DeviceIdType.MESH
BF = jnp.bfloat16
F32 = jnp.float32
LOW = 8


def up(n, m):
    return -(-n // m) * m


def dg(a, b, ca, cb):
    return lax.dot_general(a, b, (((ca,), (cb,)), ((), ())), preferred_element_type=F32)


class Plan:
    def __init__(self, nz, width, tokens, units, hidden):
        self.nz, self.width, self.tokens = nz, width, tokens
        self.lane = width // LOW
        self.block = 2 * self.lane
        self.units = units // 2
        self.hid_real = hidden // 2
        self.hid = up(self.hid_real, 16)
        self.heads = self.units // HD
        self.pieces = {}
        total = 0
        for name, rows in (
            ("n", 16),
            ("o", self.units),
            ("q", 3 * self.units),
            ("a", self.hid),
            ("b", self.hid),
            ("d", self.hid),
        ):
            self.pieces[name] = (total, rows)
            total += rows
        self.rows = total
        self.order = list(self.pieces)


def kernel(
    plan,
    x_hbm,
    dy_hbm,
    packed,
    cos_ref,
    sin_ref,
    out_hbm,
    gtok_hbm,
    gw_ref,
    W,
    xown,
    dyf,
    n1,
    qkv,
    att,
    lse,
    res,
    n2,
    AB,
    hid,
    gat,
    exs,
    exr,
    Gn,
    Gb,
    Gd,
    R1,
    R2,
    R3,
    zr,
    zs,
    xyr,
    xys,
    r1r,
    r1s,
    r2r,
    r2s,
    r3r,
    r3s,
    swr,
    sws,
    cr,
    cs,
):
    p = plan
    nz, D, T, U, H = p.nz, p.width, p.tokens, p.units, p.hid
    S = 2 * T
    L, B = p.lane, p.block
    d = lax.axis_index("dp")
    z = lax.axis_index("tensor")
    c = lax.rem(d, 2)
    r = lax.rem(d // 2, 4)
    xb = lax.rem(r, 2)
    yb = r // 2
    zb = lax.rem(z, 2)
    sib = d + 1 - 2 * c
    xp = d + 2 - 4 * xb
    yp = d + 4 - 8 * yb
    zpair = z + 1 - 2 * zb
    rx = r + 1 - 2 * xb
    ry = r + 2 - 4 * yb
    rd = 3 - r
    stay = lax.rem(c + z, 2) == 0

    def rows_at(start, n):
        return pl.ds(pl.multiple_of(start, 16), n)

    def lanes(block):
        return pl.ds(pl.multiple_of(block * B, L), B)

    mine = rows_at(c * T, T)
    theirs_start = (1 - c) * T

    def remote(src, dst, ssem, rsem, dev):
        pltpu.make_async_remote_copy(src, dst, ssem, rsem, device_id=dev, device_id_type=MESH).start()

    def take(ref, sem):
        pltpu.make_async_copy(ref, ref, sem).wait()

    partners = [(sib, z), (xp, z), (yp, z)]
    for dz in range(1, nz):
        there = lax.rem(z + dz, nz)
        partners += [(d, there), (sib, there)]
    bar = pltpu.get_barrier_semaphore()
    for dev in partners:
        pl.semaphore_signal(bar, inc=1, device_id=dev, device_id_type=MESH)
    pl.semaphore_wait(bar, len(partners))

    index = {name: i for i, name in enumerate(p.order)}

    def base(name):
        return nz * p.pieces[name][0]

    def count(name):
        return p.pieces[name][1]

    def z_start(name):
        off, n = p.pieces[name]
        i = index[name]
        dst = W.at[rows_at(base(name) + z * n, n), pl.ds(pl.multiple_of(r * B + c * L, L), L)]
        for dz in range(nz):
            there = lax.rem(z + dz, nz)
            for kk in range(2):
                k = lax.rem(c + kk, 2)
                src = packed.at[k, pl.ds(off, n), :]
                if dz == 0 and kk == 0:
                    pltpu.make_async_copy(src, dst, zr.at[i]).start()
                else:
                    remote(src, dst, zs.at[i], zr.at[i], (d if kk == 0 else sib, there))

    def half(name, which):
        n = (nz // 2) * count(name)
        return pl.ds(base(name) + which * n, n)

    def xy1(name):
        i = index[name]
        take(W.at[pl.ds(base(name), nz * count(name)), lanes(r)], zr.at[i])
        a = W.at[half(name, 0), lanes(r)]
        b = W.at[half(name, 1), lanes(r)]
        remote(a, a, xys.at[i], xyr.at[i, 0], (xp, z))
        remote(b, b, xys.at[i], xyr.at[i, 1], (yp, z))
        remote(a, a, xys.at[i], xyr.at[i, 2], (yp, z))
        remote(b, b, xys.at[i], xyr.at[i, 3], (xp, z))

    def xy2(name):
        i = index[name]
        a = W.at[half(name, 0), lanes(rx)]
        b = W.at[half(name, 1), lanes(ry)]
        take(a, xyr.at[i, 0])
        remote(a, a, xys.at[i], xyr.at[i, 4], (yp, z))
        take(b, xyr.at[i, 1])
        remote(b, b, xys.at[i], xyr.at[i, 5], (xp, z))

    def ready(name):
        i = index[name]
        take(W.at[half(name, 0), lanes(ry)], xyr.at[i, 2])
        take(W.at[half(name, 1), lanes(rx)], xyr.at[i, 3])
        take(W.at[half(name, 0), lanes(rd)], xyr.at[i, 4])
        take(W.at[half(name, 1), lanes(rd)], xyr.at[i, 5])

    def sent(name):
        i = index[name]
        n = count(name)
        take(R3.at[pl.ds(0, 2 * nz - 1), pl.ds(0, n), :], zs.at[i])
        take(W.at[pl.ds(0, 6 * (nz // 2) * n * B // D), :], xys.at[i])

    place = {
        "n": (Gn, 0),
        "q": (W, base("a")),
        "o": (W, base("a") + nz * 3 * U),
        "a": (W, base("d")),
        "b": (Gb, 0),
        "d": (Gd, 0),
    }

    def ghalf(name, which):
        n = (nz // 2) * count(name)
        return pl.ds(place[name][1] + which * n, n)

    def rhalf(name):
        return pl.ds((nz // 2) * p.pieces[name][0], (nz // 2) * count(name))

    def step_of(n):
        for s in (128, 112, 96, 80, 64, 48, 32, 16):
            if n % s == 0:
                return s
        return n

    def rs1(name):
        i = index[name]
        G = place[name][0]
        to = rhalf(name)
        for which, near, dev in ((0, ry, yp), (1, rx, xp)):
            rows = ghalf(name, which)
            remote(G.at[rows, lanes(rd)], R1.at[which, 0, to, :], r1s.at[i], r1r.at[i, which, 0], (dev, z))
        for which, near, dev in ((0, ry, yp), (1, rx, xp)):
            rows = ghalf(name, which)
            remote(G.at[rows, lanes(near)], R1.at[which, 1, to, :], r1s.at[i], r1r.at[i, which, 1], (dev, z))

    def rs2(name):
        i = index[name]
        G, gb = place[name]
        n = (nz // 2) * count(name)
        to = rhalf(name)
        s = step_of(n)
        for which, block, dev in ((0, rx, xp), (1, ry, yp)):
            take(R1.at[which, 0, to, :], r1r.at[i, which, 0])

            def add(t, _):
                g = rows_at(gb + which * n + t * s, s)
                q = rows_at(to.start + t * s, s)
                G[g, lanes(block)] = (G[g, lanes(block)].astype(F32) + R1[which, 0, q, :].astype(F32)).astype(BF)
                return 0

            lax.fori_loop(0, n // s, add, 0)
            remote(
                G.at[ghalf(name, which), lanes(block)],
                R2.at[which, to, :],
                r2s.at[i],
                r2r.at[i, which],
                (dev, z),
            )

    def rs3(name):
        i = index[name]
        G, gb = place[name]
        off, m = p.pieces[name]
        n = (nz // 2) * m
        to = rhalf(name)
        s = step_of(n)
        for which in range(2):
            take(R1.at[which, 1, to, :], r1r.at[i, which, 1])
            take(R2.at[which, to, :], r2r.at[i, which])

            def add(t, _):
                g = rows_at(gb + which * n + t * s, s)
                q = rows_at(to.start + t * s, s)
                total = G[g, lanes(r)].astype(F32) + R1[which, 1, q, :].astype(F32) + R2[which, q, :].astype(F32)
                G[g, lanes(r)] = total.astype(BF)
                return 0

            lax.fori_loop(0, n // s, add, 0)
        dst = R3.at[z * 2 + c, pl.ds(off, m), :]
        for dz in range(nz):
            there = lax.rem(z + dz, nz)
            for kk in range(2):
                k = lax.rem(c + kk, 2)
                src = G.at[rows_at(gb + there * m, m), pl.ds(pl.multiple_of(r * B + k * L, L), L)]
                if dz == 0 and kk == 0:
                    pltpu.make_async_copy(src, dst, r3r.at[i]).start()
                else:
                    remote(src, dst, r3s.at[i], r3r.at[i], (d if kk == 0 else sib, there))

    def rs4(name):
        i = index[name]
        off, m = p.pieces[name]
        take(R3.at[:, pl.ds(off, m), :], r3r.at[i])
        for k in range(2):
            total = R3[k, off : off + m, :].astype(F32)
            for j in range(1, nz):
                total += R3[2 * j + k, off : off + m, :].astype(F32)
            gw_ref[k, off : off + m, :] = total

    def rs_sent(name):
        i = index[name]
        m = count(name)
        n = (nz // 2) * m
        take(W.at[pl.ds(0, 4 * n * B // D), :], r1s.at[i])
        take(W.at[pl.ds(0, 2 * n * B // D), :], r2s.at[i])
        take(R3.at[pl.ds(0, 2 * nz - 1), pl.ds(0, m), :], r3s.at[i])

    def swap(src, dst_here, dst_there, i):
        @pl.when(stay)
        def _():
            pltpu.make_async_copy(src, dst_here, swr.at[i]).start()

        @pl.when(jnp.logical_not(stay))
        def _():
            remote(src, dst_there, sws.at[i], swr.at[i], (sib, zpair))

    def swap_sent(src, i):
        @pl.when(jnp.logical_not(stay))
        def _():
            take(src, sws.at[i])

    def give(src, dst, i):
        remote(src, dst, cs.at[i], cr.at[i], (sib, z))

    def give_rows(buf, i):
        give(buf.at[mine, :], buf.at[mine, :], i)

    def got_rows(buf, i):
        take(buf.at[mine, :], cr.at[i])

    NB = 64

    z_start("n")
    z_start("o")
    swap(x_hbm, xown, xown, 0)
    z_start("q")
    xy1("n")
    xy1("o")
    z_start("a")
    xy2("n")
    ready("n")
    swap(dy_hbm, dyf.at[mine, :], dyf.at[rows_at(theirs_start, T), :], 1)
    take(xown, swr.at[0])

    gain_one = W[0:16, :][0:1, :].astype(F32)
    gain_two = W[0:16, :][1:2, :].astype(F32)

    def norm_parts(v):
        mean = jnp.mean(v, axis=1, keepdims=True)
        cen = v - mean
        inv = lax.rsqrt(jnp.mean(cen * cen, axis=1, keepdims=True) + EPS)
        return cen, inv

    def norm_first(t, _):
        own = rows_at(t * NB, NB)
        cen, inv = norm_parts(xown[own, :].astype(F32))
        n1[rows_at(c * T + t * NB, NB), :] = (cen * inv * gain_one).astype(BF)
        return 0

    lax.fori_loop(0, T // NB, norm_first, 0)
    give_rows(n1, 0)
    xy2("o")
    xy1("q")
    z_start("b")
    got_rows(n1, 0)
    xy1("a")
    xy2("q")
    take(dyf.at[mine, :], swr.at[1])
    give_rows(dyf, 1)
    z_start("d")
    ready("q")

    TB = 256

    def project(t, _):
        zi, ti = t // (S // TB), lax.rem(t, S // TB)
        cols = pl.ds(pl.multiple_of(ti * TB, TB), TB)
        acc = dg(W[rows_at(base("q") + zi * 3 * U, 3 * U), :], n1[cols, :], 1, 1)
        co, si = cos_ref[:, cols], sin_ref[:, cols]
        parts = []
        for part in range(2):
            for h in range(p.heads):
                at = part * U + h * HD
                v1, v2 = acc[at : at + HD // 2], acc[at + HD // 2 : at + HD]
                w1, w2 = v1 * co - v2 * si, v2 * co + v1 * si
                if part == 0:
                    w1, w2 = w1 * HD**-0.5, w2 * HD**-0.5
                parts += [w1, w2]
        parts.append(acc[2 * U :])
        qkv[zi, :, cols] = jnp.concatenate(parts, axis=0).astype(BF)
        return 0

    lax.fori_loop(0, nz * (S // TB), project, 0)
    xy2("a")
    xy1("b")

    QB = 256

    def attend(t, _):
        zi, h = t // p.heads, lax.rem(t, p.heads)
        key = qkv[zi, rows_at(U + h * HD, HD), :].T
        val = qkv[zi, rows_at(2 * U + h * HD, HD), :]

        def block(b, _):
            cols = pl.ds(pl.multiple_of(b * QB, QB), QB)
            s = dg(key, qkv[zi, rows_at(h * HD, HD), cols], 1, 0)
            m = jnp.max(s, axis=0, keepdims=True)
            e = jnp.exp(s - m)
            l = jnp.sum(e, axis=0, keepdims=True)
            o = dg(val, e.astype(BF), 1, 0)
            att[rows_at(zi * U + h * HD, HD), cols] = (o / l).astype(BF)
            lse[t, :, cols] = m + jnp.log(l)
            return 0

        lax.fori_loop(0, S // QB, block, 0)
        return 0

    def attend_some(lo, hi):
        lax.fori_loop(lo, hi, attend, 0)

    NH = nz * p.heads
    attend_some(0, NH // 2)
    xy2("b")
    xy1("d")
    attend_some(NH // 2, NH)
    ready("o")

    MB = 256

    def partial(lhs_rows, rhs, start):
        cols = pl.ds(pl.multiple_of(start, MB), MB)
        total = None
        for lhs, w in zip(lhs_rows, rhs):
            term = dg(lhs(cols), w[...], 0, 0)
            total = term if total is None else total + term
        return total

    def send_partial(lhs_rows, rhs, slot, there, i):
        def some(t, _):
            exs[slot, rows_at(t * MB, MB), :] = partial(lhs_rows, rhs, theirs_start + t * MB).astype(BF)
            return 0

        lax.fori_loop(0, T // MB, some, 0)
        give(exs.at[slot], exr.at[there], i)

    w_o = W.at[pl.ds(base("o"), nz * U), :]
    w_q = W.at[pl.ds(base("q"), nz * 3 * U), :]
    w_a = W.at[pl.ds(base("a"), nz * H), :]
    w_b = W.at[pl.ds(base("b"), nz * H), :]

    lhs_att = [lambda cols: att[:, cols]]
    send_partial(lhs_att, [w_o], 0, 0, 2)

    def residual(t, _):
        own = rows_at(t * MB, MB)
        res[own, :] = xown[own, :].astype(F32) + partial(lhs_att, [w_o], c * T + t * MB)
        return 0

    lax.fori_loop(0, T // MB, residual, 0)
    take(exr.at[0], cr.at[2])

    def norm_second(t, _):
        own = rows_at(t * NB, NB)
        v = res[own, :] + exr[0, own, :].astype(F32)
        res[own, :] = v
        cen, inv = norm_parts(v)
        n2[rows_at(c * T + t * NB, NB), :] = (cen * inv * gain_two).astype(BF)
        return 0

    lax.fori_loop(0, T // NB, norm_second, 0)
    give_rows(n2, 3)
    ready("a")
    ready("b")
    got_rows(n2, 3)

    def hidden(t, _):
        zi, ti = t // (S // TB), lax.rem(t, S // TB)
        cols = pl.ds(pl.multiple_of(ti * TB, TB), TB)
        rows = rows_at(zi * H, H)
        normed = n2[cols, :]
        act = dg(W[rows_at(base("a") + zi * H, H), :], normed, 1, 1)
        gate = dg(W[rows_at(base("b") + zi * H, H), :], normed, 1, 1)
        cdf = 0.5 + 0.5 * lax.erf(act * 0.7071067811865476)
        gelu = act * cdf
        slope = cdf + act * (jnp.exp(-0.5 * act * act) * 0.3989422804014327)
        hid[rows, cols] = (gelu * gate).astype(BF)
        AB[0, rows, cols] = (slope * gate).astype(BF)
        AB[1, rows, cols] = gelu.astype(BF)
        return 0

    n_tile = nz * (S // TB)
    lax.fori_loop(0, n_tile // 2, hidden, 0)
    xy2("d")
    lax.fori_loop(n_tile // 2, n_tile, hidden, 0)
    got_rows(dyf, 1)

    def grad_of(dest, at, lhs, rhs, n, lo, hi):
        def some(t, _):
            dest[rows_at(at + t * n, n), :] = dg(lhs(rows_at(t * n, n)), rhs[...], 1, 0).astype(BF)
            return 0

        lax.fori_loop(lo, hi, some, 0)

    grad_of(Gd, 0, lambda rows: hid[rows, :], dyf, H, 0, nz)
    rs1("d")
    ready("d")

    def back_hidden(t, _):
        zi, ti = t // (S // TB), lax.rem(t, S // TB)
        cols = pl.ds(pl.multiple_of(ti * TB, TB), TB)
        rows = rows_at(zi * H, H)
        g = dg(W[rows_at(base("d") + zi * H, H), :], dyf[cols, :], 1, 1)
        AB[0, rows, cols] = (g * AB[0, rows, cols].astype(F32)).astype(BF)
        AB[1, rows, cols] = (g * AB[1, rows, cols].astype(F32)).astype(BF)
        return 0

    lax.fori_loop(0, n_tile, back_hidden, 0)

    w_d = W.at[pl.ds(base("d"), nz * H), :]
    lhs_hid = [lambda cols: hid[:, cols]]
    lhs_gp = [lambda cols: AB[0, :, cols], lambda cols: AB[1, :, cols]]
    take(exs.at[0], cs.at[2])
    send_partial(lhs_hid, [w_d], 0, 0, 4)
    take(exr.at[0], cr.at[4])

    def output(t, _):
        own = rows_at(t * MB, MB)
        total = partial(lhs_hid, [w_d], c * T + t * MB)
        xs = res[own, :] + (total + exr[0, own, :].astype(F32))
        exs[1, own, :] = xs.astype(BF)
        return 0

    lax.fori_loop(0, T // MB, output, 0)
    swap(exs.at[1], out_hbm, out_hbm, 2)

    sent("d")
    grad_of(W, base("d"), lambda rows: AB[0, rows, :], n2, H, 0, nz)
    rs1("a")
    grad_of(Gb, 0, lambda rows: AB[1, rows, :], n2, H, 0, nz)
    rs1("b")
    rs2("d")
    take(exs.at[0], cs.at[4])
    send_partial(lhs_gp, [w_a, w_b], 0, 1, 5)

    rs2("a")
    take(exr.at[1], cr.at[5])

    def grad_residual(t, carry):
        own = rows_at(t * MB, MB)
        total = partial(lhs_gp, [w_a, w_b], c * T + t * MB) + exr[1, own, :].astype(F32)
        v = res[own, :]
        cen, inv = norm_parts(v)
        hat = cen * inv
        carry = carry + jnp.sum(total * hat, axis=0, keepdims=True)
        dh = total * gain_two
        back = inv * (
            dh - jnp.mean(dh, axis=1, keepdims=True) - hat * jnp.mean(dh * hat, axis=1, keepdims=True)
        )
        g = dyf[rows_at(c * T + t * MB, MB), :].astype(F32) + back
        res[own, :] = g
        dyf[rows_at(c * T + t * MB, MB), :] = g.astype(BF)
        return carry

    take(dyf.at[mine, :], cs.at[1])
    gain_two_grad = lax.fori_loop(0, T // MB, grad_residual, jnp.zeros((1, D), F32))
    give_rows(dyf, 6)
    rs3("d")
    rs2("b")
    got_rows(dyf, 6)

    sent("o")
    sent("a")
    sent("b")

    def grad_att(t, _):
        rows = rows_at(t * U, U)
        gat[rows, :] = dg(W[rows_at(base("o") + t * U, U), :], dyf[...], 1, 1).astype(BF)
        return 0

    lax.fori_loop(0, nz, grad_att, 0)
    grad_of(W, place["o"][1], lambda rows: att[rows, :], dyf, U, 0, nz)
    rs1("o")
    rs3("a")

    def attend_back(t, _):
        zi, h = t // p.heads, lax.rem(t, p.heads)
        qr, kr, vr = (rows_at(j * U + h * HD, HD) for j in range(3))
        keyT = qkv[zi, kr, :]
        key = keyT.T
        val = qkv[zi, vr, :].T
        ar = rows_at(zi * U + h * HD, HD)

        def block(b, carry):
            dk, dv = carry
            cols = pl.ds(pl.multiple_of(b * QB, QB), QB)
            q = qkv[zi, qr, cols]
            g = gat[ar, cols]
            inner = jnp.sum(g.astype(F32) * att[ar, cols].astype(F32), axis=0, keepdims=True)
            prob = jnp.exp(dg(key, q, 1, 0) - lse[t, :, cols])
            dprob = dg(val, g, 1, 0)
            ds = (prob * (dprob - inner)).astype(BF)
            dv = dv + dg(g, prob.astype(BF), 1, 1)
            dk = dk + dg(q, ds, 1, 1)
            dq = dg(keyT, ds, 1, 0) * HD**-0.5
            co, si = cos_ref[:, cols], sin_ref[:, cols]
            g1, g2 = dq[: HD // 2], dq[HD // 2 :]
            qkv[zi, qr, cols] = jnp.concatenate([g1 * co + g2 * si, g2 * co - g1 * si], axis=0).astype(BF)
            return dk, dv

        zero = jnp.zeros((HD, S), F32)
        dk, dv = lax.fori_loop(0, S // QB, block, (zero, zero))
        g1, g2 = dk[: HD // 2], dk[HD // 2 :]
        co, si = cos_ref[...], sin_ref[...]
        qkv[zi, kr, :] = jnp.concatenate([g1 * co + g2 * si, g2 * co - g1 * si], axis=0).astype(BF)
        qkv[zi, vr, :] = dv.astype(BF)
        return 0

    quarter = NH // 4
    lax.fori_loop(0, quarter, attend_back, 0)
    rs2("o")
    rs3("b")
    lax.fori_loop(quarter, 2 * quarter, attend_back, 0)
    rs3("o")
    rs4("d")
    lax.fori_loop(2 * quarter, 3 * quarter, attend_back, 0)
    rs4("a")
    lax.fori_loop(3 * quarter, NH, attend_back, 0)

    def grad_qkv(t, _):
        W[rows_at(place["q"][1] + t * 3 * U, 3 * U), :] = dg(qkv[t, :, :], n1[...], 1, 0).astype(BF)
        return 0

    lax.fori_loop(0, nz, grad_qkv, 0)
    rs1("q")

    lhs_proj = [lambda cols: qkv[:, :, cols].reshape(nz * 3 * U, MB)]
    swap_sent(exs.at[1], 2)
    take(out_hbm, swr.at[2])
    send_partial(lhs_proj, [w_q], 1, 0, 7)
    rs4("b")
    rs2("q")
    take(exr.at[0], cr.at[7])
    take(exs.at[0], cs.at[5])

    def grad_input(t, carry):
        own = rows_at(t * MB, MB)
        total = partial(lhs_proj, [w_q], c * T + t * MB) + exr[0, own, :].astype(F32)
        cen, inv = norm_parts(xown[own, :].astype(F32))
        hat = cen * inv
        carry = carry + jnp.sum(total * hat, axis=0, keepdims=True)
        dh = total * gain_one
        back = inv * (
            dh - jnp.mean(dh, axis=1, keepdims=True) - hat * jnp.mean(dh * hat, axis=1, keepdims=True)
        )
        exs[0, own, :] = (res[own, :] + back).astype(BF)
        return carry

    gain_one_grad = lax.fori_loop(0, T // MB, grad_input, jnp.zeros((1, D), F32))
    swap(exs.at[0], gtok_hbm, gtok_hbm, 3)
    line = lax.broadcasted_iota(jnp.int32, (16, D), 0)
    both = jnp.where(line == 0, gain_one_grad, jnp.where(line == 1, gain_two_grad, 0.0)).astype(BF)
    for j in range(nz):
        Gn[16 * j : 16 * j + 16, :] = both
    rs1("n")
    rs2("n")
    rs3("q")
    rs3("n")
    rs4("o")
    rs4("q")
    rs4("n")

    sent("n")
    sent("q")
    for name in p.order:
        rs_sent(name)
    swap_sent(x_hbm, 0)
    swap_sent(dy_hbm, 1)
    swap_sent(exs.at[0], 3)
    take(gtok_hbm, swr.at[3])
    take(n1.at[mine, :], cs.at[0])
    take(n2.at[mine, :], cs.at[3])
    take(dyf.at[mine, :], cs.at[6])
    take(exs.at[1], cs.at[7])


def layer(plan, x, dy, packed, cosine, sine):
    p = plan
    nz, D, T, U, H = p.nz, p.width, p.tokens, p.units, p.hid
    S = 2 * T
    n = len(p.order)
    hbm = pl.BlockSpec(memory_space=pl.ANY)
    vmem = pl.BlockSpec(memory_space=pltpu.VMEM)
    dma = pltpu.SemaphoreType.DMA
    scratch = [
        pltpu.VMEM((nz * p.rows, D), BF),
        pltpu.VMEM((T, D), BF),
        pltpu.VMEM((S, D), BF),
        pltpu.VMEM((S, D), BF),
        pltpu.VMEM((nz, 3 * U, S), BF),
        pltpu.VMEM((nz * U, S), BF),
        pltpu.VMEM((nz * p.heads, 1, S), F32),
        pltpu.VMEM((T, D), F32),
        pltpu.VMEM((S, D), BF),
        pltpu.VMEM((2, nz * H, S), BF),
        pltpu.VMEM((nz * H, S), BF),
        pltpu.VMEM((nz * U, S), BF),
        pltpu.VMEM((2, T, D), BF),
        pltpu.VMEM((2, T, D), BF),
        pltpu.VMEM((nz * 16, D), BF),
        pltpu.VMEM((nz * H, D), BF),
        pltpu.VMEM((nz * H, D), BF),
        pltpu.VMEM((2, 2, (nz // 2) * p.rows, p.block), BF),
        pltpu.VMEM((2, (nz // 2) * p.rows, p.block), BF),
        pltpu.VMEM((2 * nz, p.rows, p.lane), BF),
        dma((n,)),
        dma((n,)),
        dma((n, 6)),
        dma((n,)),
        dma((n, 2, 2)),
        dma((n,)),
        dma((n, 2)),
        dma((n,)),
        dma((n,)),
        dma((n,)),
        dma((4,)),
        dma((4,)),
        dma((8,)),
        dma((8,)),
    ]
    return pl.pallas_call(
        functools.partial(kernel, p),
        out_shape=(
            jax.ShapeDtypeStruct((T, D), BF),
            jax.ShapeDtypeStruct((T, D), BF),
            jax.ShapeDtypeStruct((2, p.rows, p.lane), F32),
        ),
        in_specs=[hbm, hbm, hbm, vmem, vmem],
        out_specs=(hbm, hbm, vmem),
        scratch_shapes=scratch,
        compiler_params=pltpu.CompilerParams(
            collective_id=0, has_side_effects=True, vmem_limit_bytes=64 * 1024 * 1024 - 65536
        ),
        name="layer",
    )(x, dy, packed, cosine, sine)


def local(outer, nz, tokens, w_qkv, w_out, w_in, w_down, gain_attn, gain_mlp, grad_output):
    T, D = tokens.shape
    groups = [[hi * LOW + lo for hi in range(outer)] for lo in range(LOW)]
    piece = D // (outer * LOW)

    def widen(a, axis):
        if outer == 1:
            return a
        return lax.all_gather(a, "dp", axis=axis, tiled=True, axis_index_groups=groups)

    def narrow(a, axis):
        if outer == 1:
            return a
        return lax.psum_scatter(a, "dp", scatter_dimension=axis, tiled=True, axis_index_groups=groups)

    def turn(a, first, second):
        if outer == 1:
            return a
        return a.reshape(T, first, second, piece).swapaxes(1, 2).reshape(T, D)

    w_qkv, w_in = widen(w_qkv, 0), widen(w_in, 0)
    w_out, w_down = widen(w_out, 1), widen(w_down, 1)
    gains = [widen(g, 0) for g in (gain_attn, gain_mlp)]
    x = turn(tokens, outer, LOW)
    dy = turn(grad_output, outer, LOW)
    plan = Plan(nz, D, T, w_qkv.shape[2], w_in.shape[2])
    p = plan
    U, L, real, pad = p.units, p.lane, p.hid_real, p.hid - p.hid_real
    gain_rows = jnp.pad(jnp.stack(gains), ((0, 14), (0, 0)))
    gain_rows = jnp.broadcast_to(gain_rows[None], (2, 16, L))
    out_rows = w_out.reshape(2, U, L)
    qkv_rows = w_qkv.reshape(L, 3, 2, U).transpose(2, 1, 3, 0).reshape(2, 3 * U, L)
    in_rows = w_in.reshape(L, 2, 2, real).transpose(2, 1, 3, 0)
    in_rows = jnp.pad(in_rows, ((0, 0), (0, 0), (0, pad), (0, 0))).reshape(2, 2 * p.hid, L)
    down_rows = jnp.pad(w_down.reshape(2, real, L), ((0, 0), (0, pad), (0, 0)))
    packed = jnp.concatenate([gain_rows, out_rows, qkv_rows, in_rows, down_rows], axis=1)

    freq = THETA ** (-(jnp.arange(HD // 2).astype(F32) * 2.0 / HD))
    angle = freq[:, None] * jnp.arange(LEN).astype(F32)[None, :]
    out, gtok, gw = layer(plan, x, dy, packed, jnp.cos(angle), jnp.sin(angle))

    out, gtok = turn(out, LOW, outer), turn(gtok, LOW, outer)

    def rows(name):
        off, n = p.pieces[name]
        return gw[:, off : off + n, :]

    g_out = rows("o").reshape(2 * U, L)
    g_qkv = rows("q").reshape(2, 3, U, L).transpose(3, 1, 0, 2).reshape(L, 3, 2 * U)
    g_in = jnp.stack([rows("a")[:, :real], rows("b")[:, :real]]).transpose(3, 0, 1, 2).reshape(L, 2, 2 * real)
    g_down = rows("d")[:, :real].reshape(2 * real, L)
    g_gain = rows("n")[0] + rows("n")[1]
    return (
        out,
        gtok,
        narrow(g_qkv, 0),
        narrow(g_out, 1),
        narrow(g_in, 0),
        narrow(g_down, 1),
        narrow(g_gain[0], 0),
        narrow(g_gain[1], 0),
    )


def solution(mesh):
    rows = P(("dp", "tensor"), None)
    deep = P("dp", None, "tensor")
    wide = P("tensor", "dp")
    flat = P("dp")
    return jax.shard_map(
        functools.partial(local, mesh.shape["dp"] // LOW, mesh.shape["tensor"]),
        mesh=mesh,
        in_specs=(rows, deep, wide, deep, wide, flat, flat, rows),
        out_specs=(rows, rows, deep, wide, deep, wide, flat, flat),
        check_vma=False,
    )
```

time: 1330 us -> 313 us (0.24)
  waiting for transfers between devices: 989 us -> 0 us
  Pallas kernels: 0 us -> 295 us
  matrix products: 150 us -> 0 us
  other arithmetic: 64.2 us -> 3.57 us
  blocking collectives: 57.4 us -> 0 us
  between operations: 15.4 us -> 0.7 us
    reduce_scatter x8 -> x0, waiting for transfers between devices: 611 us -> none  [the longest x1 132 us: local(): lax.psum_scatter(jnp.dot(attended_b, out_w, preferred_element_type=jnp.fl...]
    all_gather x7 -> x0, waiting for transfers between devices: 377 us -> none  [the longest x1 82.9 us: local(): gathered_two = lax.all_gather(normed_two, 'tensor', axis=0, tiled=True)]
    pallas_call x0 -> x1, Pallas kernels: none -> 295 us  [layer(): pl.pallas_call(functools.partial(kernel, p), out_shape=(jax.ShapeDtypeStr...]
    dot_general x40 -> x0, matrix products: 150 us -> none  [the longest x1 13.5 us: local(): jnp.einsum('tcf,dcf->td', grad_pair, in_w, preferred_element_type=jnp.flo...]
    all_gather x3 -> x0, blocking collectives: 31.6 us -> none  [the longest x1 12.3 us: local(): lax.all_gather(w_out, 'dp', axis=1, tiled=True)]
    reduce_sum x12 -> x0, other arithmetic: 22.7 us -> none  [the longest x4 7.32 us: single(): total = jnp.sum(jnp.exp(scores - highest), axis=-1, keepdims=True)]
    broadcast_in_dim x4 -> x0, other arithmetic: 17.7 us -> none  [the longest x2 17.7 us: geglu(): return jax.nn.gelu(pair[:, 0], approximate=False) * pair[:, 1]]
    convert_element_type x11 -> x1, other arithmetic: 16.5 us -> 0.01 us  [local(): angle = freq[:, None] * jnp.arange(LEN).astype(F32)[None, :]]
  transfers between devices with their start and end apart: 15 -> 0, of which waited for: 15 -> 0; matrix products, arithmetic and copies ran while one was open for 5% -> 0% of each run, Pallas kernels for 0% -> 0%
where the time goes in v1:
time: 313 us
  Pallas kernels  295 us (94%)
  local copies, waits for them, and re-layouts  13.9 us (4%)
  other arithmetic  3.57 us (1%)
    pallas_call x1, Pallas kernels, layer(): pl.pallas_call(functools.partial(kernel, p), out_shape=(jax.ShapeDtypeStr...  295 us

profile of v1, /device:TPU:0, one launch (start us, length us, event | category | flops | bytes accessed | tf_op | source)
XLA Modules:
  0.0 312.8 jit_solution(15704052965507762369)
XLA Ops:
  0.6 0.0 copy-start.3
  0.7 0.7 fusion.2
  1.4 1.0 reshape.67
  2.4 0.0 copy-start.2
  2.4 0.2 copy.16
  2.5 1.2 multiply_sine_fusion
  3.8 1.0 copy.20
  4.8 0.6 constant_dynamic-update-slice_fusion.3
  5.4 0.0 copy-done.3
  5.4 0.6 constant_dynamic-update-slice_fusion.2
  6.1 0.7 constant_dynamic-update-slice_fusion.1
  6.8 0.8 constant_dynamic-update-slice_fusion
  7.5 0.0 copy-done.2
  7.5 0.7 pad_dynamic-update-slice_fusion.packed
  8.2 294.7 %layer.1 = (bf16[512,1024]{1,0:T(8,128)(2,1)}, bf16[512,1024]{1,0:T(8,128)(2,1)}, f32[2,1536,128]{2,1,0:T(8,128)}) custom-call(bf16[512,1024]{1,0:T(8,128)(2,1)} %x_hbm.1, bf16[512,1024]{1,0:T(8,128)(2,1)} %dy_hbm.1, bf16[2,1536,128]{2,1,0:T(8,128)(2,1)} %pad_dynamic-update-slice_fusion.packed, f32[32,1024]{1,0:T(8,128)} %get-tuple-element.20.cos_ref, ...), custom_call_target="tpu_custom_call" | custom-call | tf_op jit(solution)/shard_map/layer/pallas_call | solution.py:727
  302.9 0.7 slice_add_fusion
  303.6 0.5 slice_bitcast_fusion.2
  304.1 1.6 slice.40
  305.7 1.0 slice.39
  306.7 2.0 fusion.3
  308.7 0.0 copy-start.1
  308.7 0.2 copy.18
  308.9 1.1 reshape.73
  309.9 0.0 copy-start
  309.9 0.9 pad_maximum_fusion
  310.8 0.0 copy-done.1
  310.8 1.0 copy.27
  311.8 0.0 copy-done
  311.8 1.0 copy.28
  (3 shorter events, 0.0 us)
Async XLA Ops:
  0.6 4.8 %copy-start.3 = (bf16[256,128]{1,0:T(8,128)(2,1)S(1)}, bf16[256,128]{1,0:T(8,128)(2,1)}, u32[]{:S(2)}) copy-start(bf16[256,128]{1,0:T(8,128)(2,1)} %param.10) | copy-start | bytes 196612
  2.4 5.2 %copy-start.2 = (bf16[656,128]{1,0:T(8,128)(2,1)S(1)}, bf16[656,128]{1,0:T(8,128)(2,1)}, u32[]{:S(2)}) copy-start(bf16[656,128]{1,0:T(8,128)(2,1)} %param.12) | copy-start | bytes 503812
  308.7 2.2 copy-start.1
  309.9 1.9 copy-start

commit v2 on v1

--- a/solution.py
+++ b/solution.py
@@ -2,6 +2,7 @@
 
 import jax
 import jax.numpy as jnp
+import numpy as np
 from jax import lax
 from jax.experimental import pallas as pl
 from jax.experimental.pallas import tpu as pltpu
@@ -31,35 +32,42 @@
         self.lane = width // LOW
         self.block = 2 * self.lane
         self.units = units // 2
-        self.hid_real = hidden // 2
-        self.hid = up(self.hid_real, 16)
         self.heads = self.units // HD
+        self.real = hidden
+        self.hid = up(-(-hidden // 2), 16)
+        self.cuts = next(n for n in (3, 2, 1) if self.hid % (16 * n) == 0)
+        self.sub = self.hid // self.cuts
         self.pieces = {}
         total = 0
-        for name, rows in (
-            ("n", 16),
-            ("o", self.units),
-            ("q", 3 * self.units),
-            ("a", self.hid),
-            ("b", self.hid),
-            ("d", self.hid),
-        ):
+        sizes = [("n", 16), ("o", self.units)]
+        sizes += [(f"q{j}", 3 * HD) for j in range(self.heads)]
+        sizes += [(f"{m}{i}", self.sub) for m in "abd" for i in range(self.cuts)]
+        for name, rows in sizes:
             self.pieces[name] = (total, rows)
             total += rows
         self.rows = total
-        self.order = list(self.pieces)
+        self.order = ["n", "o"] + [f"q{j}" for j in range(self.heads)]
+        self.order += [f"{m}{i}" for i in range(self.cuts) for m in "ab"]
+        self.order += [f"d{i}" for i in range(self.cuts)]
 
 
 def kernel(
     plan,
     x_hbm,
     dy_hbm,
-    packed,
-    cos_ref,
-    sin_ref,
+    gains,
+    w_o_hbm,
+    w_q_hbm,
+    w_ab_hbm,
+    w_d_hbm,
+    rope_hbm,
     out_hbm,
     gtok_hbm,
-    gw_ref,
+    g_n_hbm,
+    g_o_hbm,
+    g_q_hbm,
+    g_ab_hbm,
+    g_d_hbm,
     W,
     xown,
     dyf,
@@ -80,6 +88,8 @@
     R1,
     R2,
     R3,
+    rope,
+    stage,
     zr,
     zs,
     xyr,
@@ -94,6 +104,7 @@
     sws,
     cr,
     cs,
+    gs,
 ):
     p = plan
     nz, D, T, U, H = p.nz, p.width, p.tokens, p.units, p.hid
@@ -139,7 +150,20 @@
         pl.semaphore_signal(bar, inc=1, device_id=dev, device_id_type=MESH)
     pl.semaphore_wait(bar, len(partners))
 
-    index = {name: i for i, name in enumerate(p.order)}
+    index = {name: i for i, name in enumerate(p.pieces)}
+    M, cuts = p.sub, p.cuts
+
+    def shard(name, k):
+        kind, j = name[0], int(name[1:] or 0)
+        if kind == "n":
+            return gains
+        if kind == "o":
+            return w_o_hbm.at[rows_at(k * U, U), :]
+        if kind == "q":
+            return w_q_hbm.at[rows_at(k * 3 * U + j * 3 * HD, 3 * HD), :]
+        if kind == "d":
+            return w_d_hbm.at[rows_at(k * H + j * M, M), :]
+        return w_ab_hbm.at[0 if kind == "a" else 1, rows_at(k * H + j * M, M), :]
 
     def base(name):
         return nz * p.pieces[name][0]
@@ -155,7 +179,7 @@
             there = lax.rem(z + dz, nz)
             for kk in range(2):
                 k = lax.rem(c + kk, 2)
-                src = packed.at[k, pl.ds(off, n), :]
+                src = shard(name, k)
                 if dz == 0 and kk == 0:
                     pltpu.make_async_copy(src, dst, zr.at[i]).start()
                 else:
@@ -197,14 +221,13 @@
         take(R3.at[pl.ds(0, 2 * nz - 1), pl.ds(0, n), :], zs.at[i])
         take(W.at[pl.ds(0, 6 * (nz // 2) * n * B // D), :], xys.at[i])
 
-    place = {
-        "n": (Gn, 0),
-        "q": (W, base("a")),
-        "o": (W, base("a") + nz * 3 * U),
-        "a": (W, base("d")),
-        "b": (Gb, 0),
-        "d": (Gd, 0),
-    }
+    place = {"n": (Gn, 0), "o": (W, base("a0") + nz * 3 * U)}
+    for j in range(p.heads):
+        place[f"q{j}"] = (W, base("a0") + j * nz * 3 * HD)
+    for i in range(cuts):
+        place[f"a{i}"] = (W, base("d0") + i * nz * M)
+        place[f"b{i}"] = (Gb, i * nz * M)
+        place[f"d{i}"] = (Gd, i * nz * M)
 
     def ghalf(name, which):
         n = (nz // 2) * count(name)
@@ -292,7 +315,35 @@
             total = R3[k, off : off + m, :].astype(F32)
             for j in range(1, nz):
                 total += R3[2 * j + k, off : off + m, :].astype(F32)
-            gw_ref[k, off : off + m, :] = total
+            stage[k, off : off + m, :] = total
+        if name == "n":
+            stage[0, off : off + m, :] += stage[1, off : off + m, :]
+        for j, (src, dst) in enumerate(stores(name)):
+            pltpu.make_async_copy(src, dst, gs.at[i, j]).start()
+
+    def stores(name):
+        off, m = p.pieces[name]
+        kind, j = name[0], int(name[1:] or 0)
+        if kind == "n":
+            return [(stage.at[0, pl.ds(off, m), :], g_n_hbm)]
+        pairs = []
+        for k in range(2):
+            n = m
+            if kind == "o":
+                dst, at = g_o_hbm, k * U
+            elif kind == "q":
+                dst, at = g_q_hbm, k * 3 * U + j * 3 * HD
+            else:
+                at = k * H + j * M
+                n = min(m, p.real - at)
+                dst = g_d_hbm if kind == "d" else g_ab_hbm.at[0 if kind == "a" else 1]
+            if n > 0:
+                pairs.append((stage.at[k, pl.ds(off, n), :], dst.at[pl.ds(at, n), :]))
+        return pairs
+
+    def stored(name):
+        for j, (src, dst) in enumerate(stores(name)):
+            take(dst, gs.at[index[name], j])
 
     def rs_sent(name):
         i = index[name]
@@ -327,16 +378,26 @@
 
     NB = 64
 
-    z_start("n")
-    z_start("o")
+    order = p.order
+    steps = iter(range(len(order) + 1))
+
+    def pump():
+        k = next(steps)
+        if k < len(order):
+            xy1(order[k])
+        if k + 2 < len(order):
+            z_start(order[k + 2])
+        if 0 < k:
+            xy2(order[k - 1])
+
+    z_start(order[0])
+    z_start(order[1])
     swap(x_hbm, xown, xown, 0)
-    z_start("q")
-    xy1("n")
-    xy1("o")
-    z_start("a")
-    xy2("n")
+    pltpu.make_async_copy(rope_hbm, rope, gs.at[len(order), 0]).start()
+    cos_ref, sin_ref = rope.at[0], rope.at[1]
+    pump()
+    pump()
     ready("n")
-    swap(dy_hbm, dyf.at[mine, :], dyf.at[rows_at(theirs_start, T), :], 1)
     take(xown, swr.at[0])
 
     gain_one = W[0:16, :][0:1, :].astype(F32)
@@ -354,72 +415,69 @@
         n1[rows_at(c * T + t * NB, NB), :] = (cen * inv * gain_one).astype(BF)
         return 0
 
+    pump()
     lax.fori_loop(0, T // NB, norm_first, 0)
     give_rows(n1, 0)
-    xy2("o")
-    xy1("q")
-    z_start("b")
+    for j in range(p.heads):
+        pump()
+    swap(dy_hbm, dyf.at[mine, :], dyf.at[rows_at(theirs_start, T), :], 1)
     got_rows(n1, 0)
-    xy1("a")
-    xy2("q")
-    take(dyf.at[mine, :], swr.at[1])
-    give_rows(dyf, 1)
-    z_start("d")
-    ready("q")
+    take(rope, gs.at[len(order), 0])
 
     TB = 256
+    QR = nz * 3 * HD
 
     def project(t, _):
-        zi, ti = t // (S // TB), lax.rem(t, S // TB)
+        j, ti = t // (S // TB), lax.rem(t, S // TB)
         cols = pl.ds(pl.multiple_of(ti * TB, TB), TB)
-        acc = dg(W[rows_at(base("q") + zi * 3 * U, 3 * U), :], n1[cols, :], 1, 1)
+        acc = dg(W[rows_at(base("q0") + j * QR, QR), :], n1[cols, :], 1, 1)
         co, si = cos_ref[:, cols], sin_ref[:, cols]
-        parts = []
-        for part in range(2):
-            for h in range(p.heads):
-                at = part * U + h * HD
+        for zi in range(nz):
+            parts = []
+            for part in range(2):
+                at = (zi * 3 + part) * HD
                 v1, v2 = acc[at : at + HD // 2], acc[at + HD // 2 : at + HD]
                 w1, w2 = v1 * co - v2 * si, v2 * co + v1 * si
                 if part == 0:
                     w1, w2 = w1 * HD**-0.5, w2 * HD**-0.5
                 parts += [w1, w2]
-        parts.append(acc[2 * U :])
-        qkv[zi, :, cols] = jnp.concatenate(parts, axis=0).astype(BF)
-        return 0
-
-    lax.fori_loop(0, nz * (S // TB), project, 0)
-    xy2("a")
-    xy1("b")
+            parts.append(acc[(zi * 3 + 2) * HD : (zi * 3 + 3) * HD])
+            qkv[rows_at(j * QR + zi * 3 * HD, 3 * HD), cols] = jnp.concatenate(parts, axis=0).astype(BF)
+        return 0
 
     QB = 256
 
+    def head_rows(t):
+        q, k, v = (rows_at((t * 3 + part) * HD, HD) for part in range(3))
+        return q, k, v, rows_at(lax.rem(t, nz) * U + t // nz * HD, HD)
+
     def attend(t, _):
-        zi, h = t // p.heads, lax.rem(t, p.heads)
-        key = qkv[zi, rows_at(U + h * HD, HD), :].T
-        val = qkv[zi, rows_at(2 * U + h * HD, HD), :]
+        q_rows, k_rows, v_rows, o_rows = head_rows(t)
+        key = qkv[k_rows, :].T
+        val = qkv[v_rows, :]
 
         def block(b, _):
             cols = pl.ds(pl.multiple_of(b * QB, QB), QB)
-            s = dg(key, qkv[zi, rows_at(h * HD, HD), cols], 1, 0)
+            s = dg(key, qkv[q_rows, cols], 1, 0)
             m = jnp.max(s, axis=0, keepdims=True)
             e = jnp.exp(s - m)
             l = jnp.sum(e, axis=0, keepdims=True)
             o = dg(val, e.astype(BF), 1, 0)
-            att[rows_at(zi * U + h * HD, HD), cols] = (o / l).astype(BF)
+            att[o_rows, cols] = (o / l).astype(BF)
             lse[t, :, cols] = m + jnp.log(l)
             return 0
 
         lax.fori_loop(0, S // QB, block, 0)
         return 0
 
-    def attend_some(lo, hi):
-        lax.fori_loop(lo, hi, attend, 0)
-
+    for j in range(p.heads):
+        ready(f"q{j}")
+        lax.fori_loop(j * (S // TB), (j + 1) * (S // TB), project, 0)
+    pump()
     NH = nz * p.heads
-    attend_some(0, NH // 2)
-    xy2("b")
-    xy1("d")
-    attend_some(NH // 2, NH)
+    for t in range(0, NH, 2):
+        lax.fori_loop(t, t + 2, attend, 0)
+        pump()
     ready("o")
 
     MB = 256
@@ -441,9 +499,10 @@
         give(exs.at[slot], exr.at[there], i)
 
     w_o = W.at[pl.ds(base("o"), nz * U), :]
-    w_q = W.at[pl.ds(base("q"), nz * 3 * U), :]
-    w_a = W.at[pl.ds(base("a"), nz * H), :]
-    w_b = W.at[pl.ds(base("b"), nz * H), :]
+    w_q = W.at[pl.ds(base("q0"), nz * 3 * U), :]
+    w_a = W.at[pl.ds(base("a0"), nz * H), :]
+    w_b = W.at[pl.ds(base("b0"), nz * H), :]
+    w_d = W.at[pl.ds(base("d0"), nz * H), :]
 
     lhs_att = [lambda cols: att[:, cols]]
     send_partial(lhs_att, [w_o], 0, 0, 2)
@@ -466,17 +525,20 @@
 
     lax.fori_loop(0, T // NB, norm_second, 0)
     give_rows(n2, 3)
-    ready("a")
-    ready("b")
+    take(dyf.at[mine, :], swr.at[1])
+    give_rows(dyf, 1)
+    pump()
     got_rows(n2, 3)
 
+    HB = nz * M
+
     def hidden(t, _):
-        zi, ti = t // (S // TB), lax.rem(t, S // TB)
+        i, ti = t // (S // TB), lax.rem(t, S // TB)
         cols = pl.ds(pl.multiple_of(ti * TB, TB), TB)
-        rows = rows_at(zi * H, H)
+        rows = rows_at(i * HB, HB)
         normed = n2[cols, :]
-        act = dg(W[rows_at(base("a") + zi * H, H), :], normed, 1, 1)
-        gate = dg(W[rows_at(base("b") + zi * H, H), :], normed, 1, 1)
+        act = dg(W[rows_at(base("a0") + i * HB, HB), :], normed, 1, 1)
+        gate = dg(W[rows_at(base("b0") + i * HB, HB), :], normed, 1, 1)
         cdf = 0.5 + 0.5 * lax.erf(act * 0.7071067811865476)
         gelu = act * cdf
         slope = cdf + act * (jnp.exp(-0.5 * act * act) * 0.3989422804014327)
@@ -485,61 +547,61 @@
         AB[1, rows, cols] = gelu.astype(BF)
         return 0
 
-    n_tile = nz * (S // TB)
-    lax.fori_loop(0, n_tile // 2, hidden, 0)
-    xy2("d")
-    lax.fori_loop(n_tile // 2, n_tile, hidden, 0)
-    got_rows(dyf, 1)
-
-    def grad_of(dest, at, lhs, rhs, n, lo, hi):
-        def some(t, _):
-            dest[rows_at(at + t * n, n), :] = dg(lhs(rows_at(t * n, n)), rhs[...], 1, 0).astype(BF)
-            return 0
-
-        lax.fori_loop(lo, hi, some, 0)
-
-    grad_of(Gd, 0, lambda rows: hid[rows, :], dyf, H, 0, nz)
-    rs1("d")
-    ready("d")
+    def grad_of(name, lhs, rhs):
+        dest, at = place[name]
+        dest[pl.ds(at, nz * p.pieces[name][1]), :] = dg(lhs, rhs[...], 1, 0).astype(BF)
+
+    for i in range(cuts):
+        ready(f"a{i}")
+        ready(f"b{i}")
+        lax.fori_loop(i * (S // TB), (i + 1) * (S // TB), hidden, 0)
+        if i == 0:
+            got_rows(dyf, 1)
+        grad_of(f"d{i}", hid[i * HB : (i + 1) * HB, :], dyf)
+        rs1(f"d{i}")
+        pump()
+    for _ in steps:
+        raise ValueError("steps left")
 
     def back_hidden(t, _):
-        zi, ti = t // (S // TB), lax.rem(t, S // TB)
+        i, ti = t // (S // TB), lax.rem(t, S // TB)
         cols = pl.ds(pl.multiple_of(ti * TB, TB), TB)
-        rows = rows_at(zi * H, H)
-        g = dg(W[rows_at(base("d") + zi * H, H), :], dyf[cols, :], 1, 1)
+        rows = rows_at(i * HB, HB)
+        g = dg(W[rows_at(base("d0") + i * HB, HB), :], dyf[cols, :], 1, 1)
         AB[0, rows, cols] = (g * AB[0, rows, cols].astype(F32)).astype(BF)
         AB[1, rows, cols] = (g * AB[1, rows, cols].astype(F32)).astype(BF)
         return 0
 
-    lax.fori_loop(0, n_tile, back_hidden, 0)
-
-    w_d = W.at[pl.ds(base("d"), nz * H), :]
+    for i in range(cuts):
+        ready(f"d{i}")
+        lax.fori_loop(i * (S // TB), (i + 1) * (S // TB), back_hidden, 0)
+        grad_of(f"b{i}", AB[1, i * HB : (i + 1) * HB, :], n2)
+        rs1(f"b{i}")
+
     lhs_hid = [lambda cols: hid[:, cols]]
     lhs_gp = [lambda cols: AB[0, :, cols], lambda cols: AB[1, :, cols]]
     take(exs.at[0], cs.at[2])
     send_partial(lhs_hid, [w_d], 0, 0, 4)
+    send_partial(lhs_gp, [w_a, w_b], 1, 1, 5)
     take(exr.at[0], cr.at[4])
+    take(exs.at[0], cs.at[4])
 
     def output(t, _):
         own = rows_at(t * MB, MB)
         total = partial(lhs_hid, [w_d], c * T + t * MB)
         xs = res[own, :] + (total + exr[0, own, :].astype(F32))
-        exs[1, own, :] = xs.astype(BF)
+        exs[0, own, :] = xs.astype(BF)
         return 0
 
     lax.fori_loop(0, T // MB, output, 0)
-    swap(exs.at[1], out_hbm, out_hbm, 2)
-
-    sent("d")
-    grad_of(W, base("d"), lambda rows: AB[0, rows, :], n2, H, 0, nz)
-    rs1("a")
-    grad_of(Gb, 0, lambda rows: AB[1, rows, :], n2, H, 0, nz)
-    rs1("b")
-    rs2("d")
-    take(exs.at[0], cs.at[4])
-    send_partial(lhs_gp, [w_a, w_b], 0, 1, 5)
-
-    rs2("a")
+    swap(exs.at[0], out_hbm, out_hbm, 2)
+
+    for i in range(cuts):
+        sent(f"d{i}")
+    for i in range(cuts):
+        grad_of(f"a{i}", AB[0, i * HB : (i + 1) * HB, :], n2)
+        rs1(f"a{i}")
+    rs2("d0")
     take(exr.at[1], cr.at[5])
 
     def grad_residual(t, carry):
@@ -561,13 +623,14 @@
     take(dyf.at[mine, :], cs.at[1])
     gain_two_grad = lax.fori_loop(0, T // MB, grad_residual, jnp.zeros((1, D), F32))
     give_rows(dyf, 6)
-    rs3("d")
-    rs2("b")
+    for i in range(1, cuts):
+        rs2(f"d{i}")
     got_rows(dyf, 6)
 
     sent("o")
-    sent("a")
-    sent("b")
+    for i in range(cuts):
+        sent(f"a{i}")
+        sent(f"b{i}")
 
     def grad_att(t, _):
         rows = rows_at(t * U, U)
@@ -575,24 +638,21 @@
         return 0
 
     lax.fori_loop(0, nz, grad_att, 0)
-    grad_of(W, place["o"][1], lambda rows: att[rows, :], dyf, U, 0, nz)
+    grad_of("o", att[...], dyf)
     rs1("o")
-    rs3("a")
 
     def attend_back(t, _):
-        zi, h = t // p.heads, lax.rem(t, p.heads)
-        qr, kr, vr = (rows_at(j * U + h * HD, HD) for j in range(3))
-        keyT = qkv[zi, kr, :]
+        q_rows, k_rows, v_rows, o_rows = head_rows(t)
+        keyT = qkv[k_rows, :]
         key = keyT.T
-        val = qkv[zi, vr, :].T
-        ar = rows_at(zi * U + h * HD, HD)
+        val = qkv[v_rows, :].T
 
         def block(b, carry):
             dk, dv = carry
             cols = pl.ds(pl.multiple_of(b * QB, QB), QB)
-            q = qkv[zi, qr, cols]
-            g = gat[ar, cols]
-            inner = jnp.sum(g.astype(F32) * att[ar, cols].astype(F32), axis=0, keepdims=True)
+            q = qkv[q_rows, cols]
+            g = gat[o_rows, cols]
+            inner = jnp.sum(g.astype(F32) * att[o_rows, cols].astype(F32), axis=0, keepdims=True)
             prob = jnp.exp(dg(key, q, 1, 0) - lse[t, :, cols])
             dprob = dg(val, g, 1, 0)
             ds = (prob * (dprob - inner)).astype(BF)
@@ -601,43 +661,44 @@
             dq = dg(keyT, ds, 1, 0) * HD**-0.5
             co, si = cos_ref[:, cols], sin_ref[:, cols]
             g1, g2 = dq[: HD // 2], dq[HD // 2 :]
-            qkv[zi, qr, cols] = jnp.concatenate([g1 * co + g2 * si, g2 * co - g1 * si], axis=0).astype(BF)
+            qkv[q_rows, cols] = jnp.concatenate([g1 * co + g2 * si, g2 * co - g1 * si], axis=0).astype(BF)
             return dk, dv
 
         zero = jnp.zeros((HD, S), F32)
         dk, dv = lax.fori_loop(0, S // QB, block, (zero, zero))
         g1, g2 = dk[: HD // 2], dk[HD // 2 :]
         co, si = cos_ref[...], sin_ref[...]
-        qkv[zi, kr, :] = jnp.concatenate([g1 * co + g2 * si, g2 * co - g1 * si], axis=0).astype(BF)
-        qkv[zi, vr, :] = dv.astype(BF)
-        return 0
-
-    quarter = NH // 4
-    lax.fori_loop(0, quarter, attend_back, 0)
+        qkv[k_rows, :] = jnp.concatenate([g1 * co + g2 * si, g2 * co - g1 * si], axis=0).astype(BF)
+        qkv[v_rows, :] = dv.astype(BF)
+        return 0
+
+    todo = [[] for _ in range(NH // 2)]
+    ab = [f"{m}{i}" for i in range(cuts) for m in "ba"]
+    ds = [f"d{i}" for i in range(cuts)]
+    for t, name in enumerate(ab):
+        todo[t * len(todo) // len(ab)].append((rs2, name))
+    for t, name in enumerate(ds):
+        todo[min(t + 1, len(todo) - 1)].append((rs3, name))
+    for t in range(0, NH, 2):
+        lax.fori_loop(t, t + 2, attend_back, 0)
+        if (t + 2) % nz == 0:
+            j = t // nz
+            grad_of(f"q{j}", qkv[j * QR : (j + 1) * QR, :], n1)
+            rs1(f"q{j}")
+        for step, name in todo[t // 2]:
+            step(name)
     rs2("o")
-    rs3("b")
-    lax.fori_loop(quarter, 2 * quarter, attend_back, 0)
-    rs3("o")
-    rs4("d")
-    lax.fori_loop(2 * quarter, 3 * quarter, attend_back, 0)
-    rs4("a")
-    lax.fori_loop(3 * quarter, NH, attend_back, 0)
-
-    def grad_qkv(t, _):
-        W[rows_at(place["q"][1] + t * 3 * U, 3 * U), :] = dg(qkv[t, :, :], n1[...], 1, 0).astype(BF)
-        return 0
-
-    lax.fori_loop(0, nz, grad_qkv, 0)
-    rs1("q")
-
-    lhs_proj = [lambda cols: qkv[:, :, cols].reshape(nz * 3 * U, MB)]
-    swap_sent(exs.at[1], 2)
+    for name in ab:
+        rs3(name)
+
+    lhs_proj = [lambda cols: qkv[:, cols]]
+    take(exs.at[1], cs.at[5])
+    send_partial(lhs_proj, [w_q], 1, 0, 7)
+    for j in range(p.heads - 1):
+        rs2(f"q{j}")
+    swap_sent(exs.at[0], 2)
     take(out_hbm, swr.at[2])
-    send_partial(lhs_proj, [w_q], 1, 0, 7)
-    rs4("b")
-    rs2("q")
     take(exr.at[0], cr.at[7])
-    take(exs.at[0], cs.at[5])
 
     def grad_input(t, carry):
         own = rows_at(t * MB, MB)
@@ -659,15 +720,19 @@
     for j in range(nz):
         Gn[16 * j : 16 * j + 16, :] = both
     rs1("n")
+    last = f"q{p.heads - 1}"
+    rs2(last)
     rs2("n")
-    rs3("q")
+    rs3("o")
+    for j in range(p.heads):
+        rs3(f"q{j}")
     rs3("n")
-    rs4("o")
-    rs4("q")
-    rs4("n")
+    for name in ds + ab + ["o"] + [f"q{j}" for j in range(p.heads)] + ["n"]:
+        rs4(name)
 
     sent("n")
-    sent("q")
+    for j in range(p.heads):
+        sent(f"q{j}")
     for name in p.order:
         rs_sent(name)
     swap_sent(x_hbm, 0)
@@ -678,22 +743,23 @@
     take(n2.at[mine, :], cs.at[3])
     take(dyf.at[mine, :], cs.at[6])
     take(exs.at[1], cs.at[7])
-
-
-def layer(plan, x, dy, packed, cosine, sine):
+    for name in p.order:
+        stored(name)
+
+
+def layer(plan, x, dy, gains, w_o, w_q, w_ab, w_d, rope):
     p = plan
     nz, D, T, U, H = p.nz, p.width, p.tokens, p.units, p.hid
-    S = 2 * T
+    S, L = 2 * T, p.lane
     n = len(p.order)
     hbm = pl.BlockSpec(memory_space=pl.ANY)
-    vmem = pl.BlockSpec(memory_space=pltpu.VMEM)
     dma = pltpu.SemaphoreType.DMA
     scratch = [
         pltpu.VMEM((nz * p.rows, D), BF),
         pltpu.VMEM((T, D), BF),
         pltpu.VMEM((S, D), BF),
         pltpu.VMEM((S, D), BF),
-        pltpu.VMEM((nz, 3 * U, S), BF),
+        pltpu.VMEM((nz * 3 * U, S), BF),
         pltpu.VMEM((nz * U, S), BF),
         pltpu.VMEM((nz * p.heads, 1, S), F32),
         pltpu.VMEM((T, D), F32),
@@ -709,6 +775,8 @@
         pltpu.VMEM((2, 2, (nz // 2) * p.rows, p.block), BF),
         pltpu.VMEM((2, (nz // 2) * p.rows, p.block), BF),
         pltpu.VMEM((2 * nz, p.rows, p.lane), BF),
+        pltpu.VMEM((2, HD // 2, S), F32),
+        pltpu.VMEM((2, p.rows, L), F32),
         dma((n,)),
         dma((n,)),
         dma((n, 6)),
@@ -723,22 +791,33 @@
         dma((4,)),
         dma((8,)),
         dma((8,)),
+        dma((n + 1, 2)),
     ]
     return pl.pallas_call(
         functools.partial(kernel, p),
         out_shape=(
             jax.ShapeDtypeStruct((T, D), BF),
             jax.ShapeDtypeStruct((T, D), BF),
-            jax.ShapeDtypeStruct((2, p.rows, p.lane), F32),
+            jax.ShapeDtypeStruct((16, L), F32),
+            jax.ShapeDtypeStruct((2 * U, L), F32),
+            jax.ShapeDtypeStruct((6 * U, L), F32),
+            jax.ShapeDtypeStruct((2, p.real, L), F32),
+            jax.ShapeDtypeStruct((p.real, L), F32),
         ),
-        in_specs=[hbm, hbm, hbm, vmem, vmem],
-        out_specs=(hbm, hbm, vmem),
+        in_specs=[hbm] * 8,
+        out_specs=(hbm,) * 7,
         scratch_shapes=scratch,
         compiler_params=pltpu.CompilerParams(
             collective_id=0, has_side_effects=True, vmem_limit_bytes=64 * 1024 * 1024 - 65536
         ),
         name="layer",
-    )(x, dy, packed, cosine, sine)
+    )(x, dy, gains, w_o, w_q, w_ab, w_d, rope)
+
+
+def rope_table():
+    freq = THETA ** (-np.arange(HD // 2) * 2.0 / HD)
+    angle = freq.astype(np.float32)[:, None] * np.arange(LEN, dtype=np.float32)[None, :]
+    return np.stack([np.cos(angle), np.sin(angle)]).astype(np.float32)
 
 
 def local(outer, nz, tokens, w_qkv, w_out, w_in, w_down, gain_attn, gain_mlp, grad_output):
@@ -766,33 +845,18 @@
     gains = [widen(g, 0) for g in (gain_attn, gain_mlp)]
     x = turn(tokens, outer, LOW)
     dy = turn(grad_output, outer, LOW)
-    plan = Plan(nz, D, T, w_qkv.shape[2], w_in.shape[2])
-    p = plan
-    U, L, real, pad = p.units, p.lane, p.hid_real, p.hid - p.hid_real
+    p = Plan(nz, D, T, w_qkv.shape[2], w_in.shape[2])
+    U, L, H, heads, real = p.units, p.lane, p.hid, p.heads, p.real
     gain_rows = jnp.pad(jnp.stack(gains), ((0, 14), (0, 0)))
-    gain_rows = jnp.broadcast_to(gain_rows[None], (2, 16, L))
-    out_rows = w_out.reshape(2, U, L)
-    qkv_rows = w_qkv.reshape(L, 3, 2, U).transpose(2, 1, 3, 0).reshape(2, 3 * U, L)
-    in_rows = w_in.reshape(L, 2, 2, real).transpose(2, 1, 3, 0)
-    in_rows = jnp.pad(in_rows, ((0, 0), (0, 0), (0, pad), (0, 0))).reshape(2, 2 * p.hid, L)
-    down_rows = jnp.pad(w_down.reshape(2, real, L), ((0, 0), (0, pad), (0, 0)))
-    packed = jnp.concatenate([gain_rows, out_rows, qkv_rows, in_rows, down_rows], axis=1)
-
-    freq = THETA ** (-(jnp.arange(HD // 2).astype(F32) * 2.0 / HD))
-    angle = freq[:, None] * jnp.arange(LEN).astype(F32)[None, :]
-    out, gtok, gw = layer(plan, x, dy, packed, jnp.cos(angle), jnp.sin(angle))
+    qkv_rows = w_qkv.reshape(L, 3, 2, heads, HD).transpose(2, 3, 1, 4, 0).reshape(6 * U, L)
+    in_rows = jnp.pad(w_in.transpose(1, 2, 0), ((0, 0), (0, 2 * H - real), (0, 0)))
+    down_rows = jnp.pad(w_down, ((0, 2 * H - real), (0, 0)))
+    rope = jnp.asarray(rope_table())
+    out, gtok, g_n, g_out, g_q, g_ab, g_down = layer(p, x, dy, gain_rows, w_out, qkv_rows, in_rows, down_rows, rope)
 
     out, gtok = turn(out, LOW, outer), turn(gtok, LOW, outer)
-
-    def rows(name):
-        off, n = p.pieces[name]
-        return gw[:, off : off + n, :]
-
-    g_out = rows("o").reshape(2 * U, L)
-    g_qkv = rows("q").reshape(2, 3, U, L).transpose(3, 1, 0, 2).reshape(L, 3, 2 * U)
-    g_in = jnp.stack([rows("a")[:, :real], rows("b")[:, :real]]).transpose(3, 0, 1, 2).reshape(L, 2, 2 * real)
-    g_down = rows("d")[:, :real].reshape(2 * real, L)
-    g_gain = rows("n")[0] + rows("n")[1]
+    g_qkv = g_q.reshape(2, heads, 3, HD, L).transpose(4, 2, 0, 1, 3).reshape(L, 3, 2 * U)
+    g_in = g_ab.transpose(2, 0, 1)
     return (
         out,
         gtok,
@@ -800,8 +864,8 @@
         narrow(g_out, 1),
         narrow(g_in, 0),
         narrow(g_down, 1),
-        narrow(g_gain[0], 0),
-        narrow(g_gain[1], 0),
+        narrow(g_n[0], 0),
+        narrow(g_n[1], 0),
     )
 
 

time: 313 us -> 284 us (0.907)
  Pallas kernels: 295 us -> 270 us
    pallas_call x1, Pallas kernels: 295 us -> 270 us  [layer(): pl.pallas_call(functools.partial(kernel, p), out_shape=(jax.ShapeDtypeStr...]
    slice x3 -> x0, local copies, waits for them, and re-layouts: 4.57 us -> none  [the longest x2 2.59 us: rows(): return gw[:, off:off + n, :]]
    unnamed x14 -> x25, local copies, waits for them, and re-layouts: 4.64 us -> 8.15 us
where the time goes in v2:
time: 284 us
  Pallas kernels  270 us (95%)
  local copies, waits for them, and re-layouts  12.6 us (4%)
    pallas_call x1, Pallas kernels, layer(): pl.pallas_call(functools.partial(kernel, p), out_shape=(jax.ShapeDtypeStr...  270 us
    unnamed x25, local copies, waits for them, and re-layouts  8.15 us

profile of v2, /device:TPU:0, one launch (start us, length us, event | category | flops | bytes accessed | tf_op | source)
XLA Modules:
  0.0 283.7 jit_solution(18196829223960258844)
XLA Ops:
  0.6 0.0 copy-start.3
  0.6 1.1 copy.19
  1.8 0.7 copy.20
  2.5 0.0 copy-done.3
  2.5 0.0 copy-start.5
  2.5 0.8 pad.13.w_ab_hbm
  3.2 0.3 copy-done.5
  3.5 0.7 pad.14.w_d_hbm
  4.2 0.0 copy-start.7
  4.2 0.0 copy-start.8
  4.2 0.7 copy-done.7
  4.8 0.0 copy-done.8
  4.8 0.6 fusion.2.gains
  5.4 269.8 %layer.1 = (bf16[512,1024]{1,0:T(8,128)(2,1)}, bf16[512,1024]{1,0:T(8,128)(2,1)}, f32[16,128]{1,0:T(8,128)}, f32[256,128]{1,0:T(8,128)}, f32[768,128]{1,0:T(8,12...) custom-call(bf16[512,1024]{1,0:T(8,128)(2,1)} %x_hbm.1, bf16[512,1024]{1,0:T(8,128)(2,1)} %dy_hbm.1, ...), custom_call_target="tpu_custom_call" | custom-call | tf_op jit(solution)/shard_map/layer/pallas_call | solution.py:796
  275.3 0.0 copy-start.1
  275.3 1.3 slice_bitcast_fusion
  276.6 1.0 copy.21
  277.6 0.9 copy.22
  278.5 0.0 copy-done.1
  278.5 0.0 copy-start
  278.5 1.0 copy.28
  279.5 0.6 copy-done
  280.1 0.0 copy-start.6
  280.1 0.0 copy-start.2
  280.1 1.0 copy.29
  281.1 0.0 copy-done.6
  281.1 0.7 copy.30
  281.8 0.0 copy-done.2
  281.8 0.0 copy-start.4
  281.8 0.8 copy.31
  282.6 0.3 copy-done.4
  283.0 0.7 copy.32
Async XLA Ops:
  0.6 1.8 copy-start.3
  2.5 1.0 copy-start.5
  4.2 0.7 copy-start.7
  4.2 0.7 copy-start.8
  275.3 3.2 %copy-start.1 = (bf16[512,1024]{1,0:T(8,128)(2,1)S(1)}, bf16[512,1024]{1,0:T(8,128)(2,1)}, u32[]{:S(2)}) copy-start(bf16[512,1024]{1,0:T(8,128)(2,1)} %get-tuple-element.40) | copy-start | bytes 3145732
  278.5 1.6 copy-start
  280.1 1.0 copy-start.6
  280.1 1.7 copy-start.2
  281.8 1.2 copy-start.4

commit v3 on v2

--- a/solution.py
+++ b/solution.py
@@ -15,6 +15,7 @@
 MESH = pl.DeviceIdType.MESH
 BF = jnp.bfloat16
 F32 = jnp.float32
+VMEM = 64 * 1024 * 1024 - 65536
 LOW = 8
 
 
@@ -49,13 +50,16 @@
         self.order = ["n", "o"] + [f"q{j}" for j in range(self.heads)]
         self.order += [f"{m}{i}" for i in range(self.cuts) for m in "ab"]
         self.order += [f"d{i}" for i in range(self.cuts)]
+        self.late = self.order[-1:] if self.cuts > 1 else []
+        self.early = [f"d{i}" for i in range(len(self.late))]
 
 
 def kernel(
     plan,
     x_hbm,
     dy_hbm,
-    gains,
+    gain_a_hbm,
+    gain_m_hbm,
     w_o_hbm,
     w_q_hbm,
     w_ab_hbm,
@@ -88,8 +92,16 @@
     R1,
     R2,
     R3,
+    RZ,
     rope,
     stage,
+    gains,
+    gain_rows,
+    w_q_in,
+    w_q,
+    w_ab,
+    w_d,
+    g_q,
     zr,
     zs,
     xyr,
@@ -105,6 +117,11 @@
     cr,
     cs,
     gs,
+    lr,
+    ls,
+    er,
+    es,
+    ins,
 ):
     p = plan
     nz, D, T, U, H = p.nz, p.width, p.tokens, p.units, p.hid
@@ -148,6 +165,39 @@
     bar = pltpu.get_barrier_semaphore()
     for dev in partners:
         pl.semaphore_signal(bar, inc=1, device_id=dev, device_id_type=MESH)
+
+    def load(src, dst, i):
+        return pltpu.make_async_copy(src, dst, ins.at[i])
+
+    real = p.real
+    loads = [
+        load(gain_a_hbm, gains.at[0], 0),
+        load(gain_m_hbm, gains.at[1], 1),
+        load(w_q_hbm, w_q_in, 2),
+        load(w_ab_hbm.at[0], w_ab.at[0, pl.ds(0, real), :], 3),
+        load(w_ab_hbm.at[1], w_ab.at[1, pl.ds(0, real), :], 4),
+        load(w_d_hbm, w_d.at[pl.ds(0, real), :], 5),
+        load(rope_hbm, rope, 6),
+    ]
+    for copy in loads:
+        copy.start()
+    if 2 * H > real:
+        zeros = jnp.zeros((2 * H - real, L), BF)
+        w_ab[0, real:, :] = zeros
+        w_ab[1, real:, :] = zeros
+        w_d[real:, :] = zeros
+    for copy in loads:
+        copy.wait()
+    line = lax.broadcasted_iota(jnp.int32, (16, L), 0)
+    first, second = (gains[j, :, :].astype(F32) for j in range(2))
+    gain_rows[...] = jnp.where(line == 0, first, jnp.where(line == 1, second, 0.0)).astype(BF)
+    for part in range(3):
+        turned = w_q_in[part, :, :].T
+        for k in range(2):
+            for j in range(p.heads):
+                at = k * U + j * HD
+                to = (k * p.heads + j) * 3 * HD + part * HD
+                w_q[to : to + HD, :] = turned[at : at + HD, :]
     pl.semaphore_wait(bar, len(partners))
 
     index = {name: i for i, name in enumerate(p.pieces)}
@@ -156,14 +206,14 @@
     def shard(name, k):
         kind, j = name[0], int(name[1:] or 0)
         if kind == "n":
-            return gains
+            return gain_rows
         if kind == "o":
             return w_o_hbm.at[rows_at(k * U, U), :]
         if kind == "q":
-            return w_q_hbm.at[rows_at(k * 3 * U + j * 3 * HD, 3 * HD), :]
+            return w_q.at[rows_at(k * 3 * U + j * 3 * HD, 3 * HD), :]
         if kind == "d":
-            return w_d_hbm.at[rows_at(k * H + j * M, M), :]
-        return w_ab_hbm.at[0 if kind == "a" else 1, rows_at(k * H + j * M, M), :]
+            return w_d.at[rows_at(k * H + j * M, M), :]
+        return w_ab.at[0 if kind == "a" else 1, rows_at(k * H + j * M, M), :]
 
     def base(name):
         return nz * p.pieces[name][0]
@@ -185,6 +235,48 @@
                 else:
                     remote(src, dst, zs.at[i], zr.at[i], (d if kk == 0 else sib, there))
 
+    def part(block, which):
+        return pl.ds(pl.multiple_of(block * B + which * L, L), L)
+
+    def own_rows(name):
+        n = count(name)
+        return rows_at(base(name) + z * n, n)
+
+    def late0(name):
+        i = index[name]
+        dst = W.at[own_rows(name), part(r, c)]
+        pltpu.make_async_copy(shard(name, c), dst, zr.at[i]).start()
+        remote(shard(name, 1 - c), dst, zs.at[i], zr.at[i], (sib, z))
+
+    def late1(name):
+        i = index[name]
+        own = own_rows(name)
+        take(W.at[own, lanes(r)], zr.at[i])
+        a = W.at[own, part(r, 0)]
+        b = W.at[own, part(r, 1)]
+        remote(a, a, xys.at[i], xyr.at[i, 0], (xp, z))
+        remote(b, b, xys.at[i], xyr.at[i, 1], (yp, z))
+        remote(a, a, xys.at[i], xyr.at[i, 2], (yp, z))
+        remote(b, b, xys.at[i], xyr.at[i, 3], (xp, z))
+
+    def late2(name):
+        i = index[name]
+        own = own_rows(name)
+        a = W.at[own, part(rx, 0)]
+        b = W.at[own, part(ry, 1)]
+        take(a, xyr.at[i, 0])
+        remote(a, a, xys.at[i], xyr.at[i, 4], (yp, z))
+        take(b, xyr.at[i, 1])
+        remote(b, b, xys.at[i], xyr.at[i, 5], (xp, z))
+
+    def late3(name):
+        i = index[name]
+        own = own_rows(name)
+        for slot, (block, which) in enumerate(((ry, 0), (rx, 1), (rd, 0), (rd, 1))):
+            take(W.at[own, part(block, which)], xyr.at[i, 2 + slot])
+        for dz in range(1, nz):
+            remote(W.at[own, :], W.at[own, :], ls.at[i], lr.at[i], (d, lax.rem(z + dz, nz)))
+
     def half(name, which):
         n = (nz // 2) * count(name)
         return pl.ds(base(name) + which * n, n)
@@ -210,6 +302,9 @@
 
     def ready(name):
         i = index[name]
+        if name in p.late:
+            take(W.at[pl.ds(0, (nz - 1) * count(name)), :], lr.at[i])
+            return
         take(W.at[half(name, 0), lanes(ry)], xyr.at[i, 2])
         take(W.at[half(name, 1), lanes(rx)], xyr.at[i, 3])
         take(W.at[half(name, 0), lanes(rd)], xyr.at[i, 4])
@@ -218,6 +313,11 @@
     def sent(name):
         i = index[name]
         n = count(name)
+        if name in p.late:
+            take(R3.at[0, pl.ds(0, n), :], zs.at[i])
+            take(R3.at[pl.ds(0, 6), pl.ds(0, n), :], xys.at[i])
+            take(W.at[pl.ds(0, (nz - 1) * n), :], ls.at[i])
+            return
         take(R3.at[pl.ds(0, 2 * nz - 1), pl.ds(0, n), :], zs.at[i])
         take(W.at[pl.ds(0, 6 * (nz // 2) * n * B // D), :], xys.at[i])
 
@@ -318,21 +418,108 @@
             stage[k, off : off + m, :] = total
         if name == "n":
             stage[0, off : off + m, :] += stage[1, off : off + m, :]
+        if name[0] != "q":
+            store(name)
+
+    def store(name):
         for j, (src, dst) in enumerate(stores(name)):
-            pltpu.make_async_copy(src, dst, gs.at[i, j]).start()
+            pltpu.make_async_copy(src, dst, gs.at[index[name], j]).start()
+
+    def early1(name):
+        i = index[name]
+        G, gb = place[name]
+        n = count(name)
+        at = p.early.index(name) * n
+        for dz in range(1, nz):
+            there = lax.rem(z + dz, nz)
+            src = G.at[rows_at(gb + there * n, n), :]
+            remote(src, RZ.at[dz - 1, pl.ds(at, n), :], es.at[i], er.at[i], (d, there))
+
+    def early2(name):
+        i = index[name]
+        G, gb = place[name]
+        off, n = p.pieces[name]
+        at = p.early.index(name) * n
+        take(RZ.at[:, pl.ds(at, n), :], er.at[i])
+
+        def add(t, _):
+            g = rows_at(gb + z * n + t * 16, 16)
+            q = rows_at(at + t * 16, 16)
+            total = G[g, :].astype(F32)
+            for j in range(nz - 1):
+                total += RZ[j, q, :].astype(F32)
+            G[g, :] = total.astype(BF)
+            return 0
+
+        lax.fori_loop(0, n // 16, add, 0)
+        own = rows_at(gb + z * n, n)
+        to = pl.ds(off, n)
+        for slot, (block, which, dev) in enumerate(((rd, 0, yp), (ry, 0, yp), (rd, 1, xp), (rx, 1, xp))):
+            remote(
+                G.at[own, part(block, which)],
+                R3.at[slot, to, :],
+                r1s.at[i],
+                r1r.at[i, which, slot % 2],
+                (dev, z),
+            )
+
+    def early3(name):
+        i = index[name]
+        G, gb = place[name]
+        off, n = p.pieces[name]
+        own, to = rows_at(gb + z * n, n), pl.ds(off, n)
+        for which, block, dev in ((0, rx, xp), (1, ry, yp)):
+            take(R3.at[2 * which, to, :], r1r.at[i, which, 0])
+            there = part(block, which)
+            G[own, there] = (G[own, there].astype(F32) + R3[2 * which, to, :].astype(F32)).astype(BF)
+            remote(G.at[own, there], R3.at[4 + which, to, :], r2s.at[i], r2r.at[i, which], (dev, z))
+
+    def early4(name):
+        i = index[name]
+        G, gb = place[name]
+        off, n = p.pieces[name]
+        own, to = rows_at(gb + z * n, n), pl.ds(off, n)
+        for which in range(2):
+            take(R3.at[2 * which + 1, to, :], r1r.at[i, which, 1])
+            take(R3.at[4 + which, to, :], r2r.at[i, which])
+            total = G[own, part(r, which)].astype(F32) + R3[2 * which + 1, to, :].astype(F32)
+            total += R3[4 + which, to, :].astype(F32)
+
+            @pl.when(c == which)
+            def _():
+                stage[which, to, :] = total
+
+            @pl.when(c != which)
+            def _():
+                R3[7, to, :] = total.astype(BF)
+
+        remote(R3.at[7, to, :], R3.at[6, to, :], r3s.at[i], r3r.at[i], (sib, z))
+
+    def early5(name):
+        i = index[name]
+        off, n = p.pieces[name]
+        to = pl.ds(off, n)
+        take(R3.at[6, to, :], r3r.at[i])
+        for k in range(2):
+
+            @pl.when(c != k)
+            def _():
+                stage[k, to, :] = R3[6, to, :].astype(F32)
+
+        store(name)
 
     def stores(name):
         off, m = p.pieces[name]
         kind, j = name[0], int(name[1:] or 0)
         if kind == "n":
             return [(stage.at[0, pl.ds(off, m), :], g_n_hbm)]
+        if kind == "q":
+            return [(g_q, g_q_hbm)] if j == p.heads - 1 else []
         pairs = []
         for k in range(2):
             n = m
             if kind == "o":
                 dst, at = g_o_hbm, k * U
-            elif kind == "q":
-                dst, at = g_q_hbm, k * 3 * U + j * 3 * HD
             else:
                 at = k * H + j * M
                 n = min(m, p.real - at)
@@ -348,6 +535,12 @@
     def rs_sent(name):
         i = index[name]
         m = count(name)
+        if name in p.early:
+            take(W.at[pl.ds(0, (nz - 1) * m), :], es.at[i])
+            take(R3.at[pl.ds(0, 4), pl.ds(0, m), :], r1s.at[i])
+            take(R3.at[pl.ds(0, 2), pl.ds(0, m), :], r2s.at[i])
+            take(R3.at[0, pl.ds(0, m), :], r3s.at[i])
+            return
         n = (nz // 2) * m
         take(W.at[pl.ds(0, 4 * n * B // D), :], r1s.at[i])
         take(W.at[pl.ds(0, 2 * n * B // D), :], r2s.at[i])
@@ -378,25 +571,30 @@
 
     NB = 64
 
-    order = p.order
+    order = [name for name in p.order if name not in p.late]
     steps = iter(range(len(order) + 1))
 
     def pump():
         k = next(steps)
         if k < len(order):
             xy1(order[k])
-        if k + 2 < len(order):
-            z_start(order[k + 2])
+        if k + 3 < len(order):
+            z_start(order[k + 3])
         if 0 < k:
             xy2(order[k - 1])
 
-    z_start(order[0])
-    z_start(order[1])
+    for name in p.late:
+        late0(name)
+    for name in order[:3]:
+        z_start(name)
+    for name in p.late:
+        late1(name)
     swap(x_hbm, xown, xown, 0)
-    pltpu.make_async_copy(rope_hbm, rope, gs.at[len(order), 0]).start()
     cos_ref, sin_ref = rope.at[0], rope.at[1]
     pump()
     pump()
+    for name in p.late:
+        late2(name)
     ready("n")
     take(xown, swr.at[0])
 
@@ -422,7 +620,6 @@
         pump()
     swap(dy_hbm, dyf.at[mine, :], dyf.at[rows_at(theirs_start, T), :], 1)
     got_rows(n1, 0)
-    take(rope, gs.at[len(order), 0])
 
     TB = 256
     QR = nz * 3 * HD
@@ -475,9 +672,13 @@
         lax.fori_loop(j * (S // TB), (j + 1) * (S // TB), project, 0)
     pump()
     NH = nz * p.heads
+    late = iter(p.late)
     for t in range(0, NH, 2):
         lax.fori_loop(t, t + 2, attend, 0)
         pump()
+        for name in late:
+            late3(name)
+            break
     ready("o")
 
     MB = 256
@@ -498,18 +699,18 @@
         lax.fori_loop(0, T // MB, some, 0)
         give(exs.at[slot], exr.at[there], i)
 
-    w_o = W.at[pl.ds(base("o"), nz * U), :]
-    w_q = W.at[pl.ds(base("q0"), nz * 3 * U), :]
-    w_a = W.at[pl.ds(base("a0"), nz * H), :]
-    w_b = W.at[pl.ds(base("b0"), nz * H), :]
-    w_d = W.at[pl.ds(base("d0"), nz * H), :]
+    full_o = W.at[pl.ds(base("o"), nz * U), :]
+    full_q = W.at[pl.ds(base("q0"), nz * 3 * U), :]
+    full_a = W.at[pl.ds(base("a0"), nz * H), :]
+    full_b = W.at[pl.ds(base("b0"), nz * H), :]
+    full_d = W.at[pl.ds(base("d0"), nz * H), :]
 
     lhs_att = [lambda cols: att[:, cols]]
-    send_partial(lhs_att, [w_o], 0, 0, 2)
+    send_partial(lhs_att, [full_o], 0, 0, 2)
 
     def residual(t, _):
         own = rows_at(t * MB, MB)
-        res[own, :] = xown[own, :].astype(F32) + partial(lhs_att, [w_o], c * T + t * MB)
+        res[own, :] = xown[own, :].astype(F32) + partial(lhs_att, [full_o], c * T + t * MB)
         return 0
 
     lax.fori_loop(0, T // MB, residual, 0)
@@ -547,6 +748,21 @@
         AB[1, rows, cols] = gelu.astype(BF)
         return 0
 
+    ds = [f"d{i}" for i in range(cuts) if f"d{i}" not in p.early]
+    ab = [f"{m}{i}" for m in "ba" for i in range(cuts)]
+    turn = ds + ab + ["o"] + [f"q{j}" for j in range(p.heads)] + ["n"]
+    turns = iter(range(len(turn) + 2))
+
+    def sum_next(count=1):
+        for _ in range(count):
+            k = next(turns)
+            if k < len(turn):
+                rs1(turn[k])
+            if 0 < k <= len(turn):
+                rs2(turn[k - 1])
+            if 1 < k:
+                rs3(turn[k - 2])
+
     def grad_of(name, lhs, rhs):
         dest, at = place[name]
         dest[pl.ds(at, nz * p.pieces[name][1]), :] = dg(lhs, rhs[...], 1, 0).astype(BF)
@@ -558,8 +774,12 @@
         if i == 0:
             got_rows(dyf, 1)
         grad_of(f"d{i}", hid[i * HB : (i + 1) * HB, :], dyf)
-        rs1(f"d{i}")
-        pump()
+        if f"d{i}" in p.early:
+            early1(f"d{i}")
+        else:
+            sum_next()
+        if i < 2:
+            pump()
     for _ in steps:
         raise ValueError("steps left")
 
@@ -576,19 +796,21 @@
         ready(f"d{i}")
         lax.fori_loop(i * (S // TB), (i + 1) * (S // TB), back_hidden, 0)
         grad_of(f"b{i}", AB[1, i * HB : (i + 1) * HB, :], n2)
-        rs1(f"b{i}")
+        if i == 0:
+            sum_next()
 
     lhs_hid = [lambda cols: hid[:, cols]]
     lhs_gp = [lambda cols: AB[0, :, cols], lambda cols: AB[1, :, cols]]
     take(exs.at[0], cs.at[2])
-    send_partial(lhs_hid, [w_d], 0, 0, 4)
-    send_partial(lhs_gp, [w_a, w_b], 1, 1, 5)
+    send_partial(lhs_hid, [full_d], 0, 0, 4)
+    send_partial(lhs_gp, [full_a, full_b], 1, 1, 5)
+    sum_next()
     take(exr.at[0], cr.at[4])
     take(exs.at[0], cs.at[4])
 
     def output(t, _):
         own = rows_at(t * MB, MB)
-        total = partial(lhs_hid, [w_d], c * T + t * MB)
+        total = partial(lhs_hid, [full_d], c * T + t * MB)
         xs = res[own, :] + (total + exr[0, own, :].astype(F32))
         exs[0, own, :] = xs.astype(BF)
         return 0
@@ -600,13 +822,12 @@
         sent(f"d{i}")
     for i in range(cuts):
         grad_of(f"a{i}", AB[0, i * HB : (i + 1) * HB, :], n2)
-        rs1(f"a{i}")
-    rs2("d0")
+    sum_next()
     take(exr.at[1], cr.at[5])
 
     def grad_residual(t, carry):
         own = rows_at(t * MB, MB)
-        total = partial(lhs_gp, [w_a, w_b], c * T + t * MB) + exr[1, own, :].astype(F32)
+        total = partial(lhs_gp, [full_a, full_b], c * T + t * MB) + exr[1, own, :].astype(F32)
         v = res[own, :]
         cen, inv = norm_parts(v)
         hat = cen * inv
@@ -623,8 +844,9 @@
     take(dyf.at[mine, :], cs.at[1])
     gain_two_grad = lax.fori_loop(0, T // MB, grad_residual, jnp.zeros((1, D), F32))
     give_rows(dyf, 6)
-    for i in range(1, cuts):
-        rs2(f"d{i}")
+    sum_next()
+    for name in p.early:
+        early2(name)
     got_rows(dyf, 6)
 
     sent("o")
@@ -639,7 +861,9 @@
 
     lax.fori_loop(0, nz, grad_att, 0)
     grad_of("o", att[...], dyf)
-    rs1("o")
+    sum_next()
+    for name in p.early:
+        early3(name)
 
     def attend_back(t, _):
         q_rows, k_rows, v_rows, o_rows = head_rows(t)
@@ -672,37 +896,26 @@
         qkv[v_rows, :] = dv.astype(BF)
         return 0
 
-    todo = [[] for _ in range(NH // 2)]
-    ab = [f"{m}{i}" for i in range(cuts) for m in "ba"]
-    ds = [f"d{i}" for i in range(cuts)]
-    for t, name in enumerate(ab):
-        todo[t * len(todo) // len(ab)].append((rs2, name))
-    for t, name in enumerate(ds):
-        todo[min(t + 1, len(todo) - 1)].append((rs3, name))
     for t in range(0, NH, 2):
         lax.fori_loop(t, t + 2, attend_back, 0)
         if (t + 2) % nz == 0:
             j = t // nz
             grad_of(f"q{j}", qkv[j * QR : (j + 1) * QR, :], n1)
-            rs1(f"q{j}")
-        for step, name in todo[t // 2]:
-            step(name)
-    rs2("o")
-    for name in ab:
-        rs3(name)
+        sum_next()
+        if t == 0:
+            for name in p.early:
+                early4(name)
 
     lhs_proj = [lambda cols: qkv[:, cols]]
     take(exs.at[1], cs.at[5])
-    send_partial(lhs_proj, [w_q], 1, 0, 7)
-    for j in range(p.heads - 1):
-        rs2(f"q{j}")
+    send_partial(lhs_proj, [full_q], 1, 0, 7)
     swap_sent(exs.at[0], 2)
     take(out_hbm, swr.at[2])
     take(exr.at[0], cr.at[7])
 
     def grad_input(t, carry):
         own = rows_at(t * MB, MB)
-        total = partial(lhs_proj, [w_q], c * T + t * MB) + exr[0, own, :].astype(F32)
+        total = partial(lhs_proj, [full_q], c * T + t * MB) + exr[0, own, :].astype(F32)
         cen, inv = norm_parts(xown[own, :].astype(F32))
         hat = cen * inv
         carry = carry + jnp.sum(total * hat, axis=0, keepdims=True)
@@ -719,16 +932,20 @@
     both = jnp.where(line == 0, gain_one_grad, jnp.where(line == 1, gain_two_grad, 0.0)).astype(BF)
     for j in range(nz):
         Gn[16 * j : 16 * j + 16, :] = both
-    rs1("n")
-    last = f"q{p.heads - 1}"
-    rs2(last)
-    rs2("n")
-    rs3("o")
-    for j in range(p.heads):
-        rs3(f"q{j}")
-    rs3("n")
-    for name in ds + ab + ["o"] + [f"q{j}" for j in range(p.heads)] + ["n"]:
+    sum_next(3)
+    for _ in turns:
+        raise ValueError("turns left")
+    for name in p.early:
+        early5(name)
+    for name in turn:
         rs4(name)
+    for part in range(3):
+        for k in range(2):
+            firsts = [p.pieces[f"q{j}"][0] + part * HD for j in range(p.heads)]
+            g_q[part, :, k * U : (k + 1) * U] = jnp.concatenate(
+                [stage[k, at : at + HD, :] for at in firsts], axis=0
+            ).T
+    store(f"q{p.heads - 1}")
 
     sent("n")
     for j in range(p.heads):
@@ -747,7 +964,7 @@
         stored(name)
 
 
-def layer(plan, x, dy, gains, w_o, w_q, w_ab, w_d, rope):
+def layer(plan, x, dy, gain_a, gain_m, w_o, w_q, w_ab, w_d, rope):
     p = plan
     nz, D, T, U, H = p.nz, p.width, p.tokens, p.units, p.hid
     S, L = 2 * T, p.lane
@@ -775,8 +992,16 @@
         pltpu.VMEM((2, 2, (nz // 2) * p.rows, p.block), BF),
         pltpu.VMEM((2, (nz // 2) * p.rows, p.block), BF),
         pltpu.VMEM((2 * nz, p.rows, p.lane), BF),
+        pltpu.VMEM((nz - 1, max(len(p.early), 1) * p.sub, D), BF),
         pltpu.VMEM((2, HD // 2, S), F32),
         pltpu.VMEM((2, p.rows, L), F32),
+        pltpu.VMEM((2, 1, L), BF),
+        pltpu.VMEM((16, L), BF),
+        pltpu.VMEM((3, L, 2 * U), BF),
+        pltpu.VMEM((6 * U, L), BF),
+        pltpu.VMEM((2, 2 * H, L), BF),
+        pltpu.VMEM((2 * H, L), BF),
+        pltpu.VMEM((3, L, 2 * U), F32),
         dma((n,)),
         dma((n,)),
         dma((n, 6)),
@@ -791,7 +1016,12 @@
         dma((4,)),
         dma((8,)),
         dma((8,)),
-        dma((n + 1, 2)),
+        dma((n, 2)),
+        dma((n,)),
+        dma((n,)),
+        dma((n,)),
+        dma((n,)),
+        dma((7,)),
     ]
     return pl.pallas_call(
         functools.partial(kernel, p),
@@ -800,18 +1030,55 @@
             jax.ShapeDtypeStruct((T, D), BF),
             jax.ShapeDtypeStruct((16, L), F32),
             jax.ShapeDtypeStruct((2 * U, L), F32),
-            jax.ShapeDtypeStruct((6 * U, L), F32),
+            jax.ShapeDtypeStruct((3, L, 2 * U), F32),
             jax.ShapeDtypeStruct((2, p.real, L), F32),
             jax.ShapeDtypeStruct((p.real, L), F32),
         ),
-        in_specs=[hbm] * 8,
+        in_specs=[hbm] * 9,
         out_specs=(hbm,) * 7,
         scratch_shapes=scratch,
         compiler_params=pltpu.CompilerParams(
-            collective_id=0, has_side_effects=True, vmem_limit_bytes=64 * 1024 * 1024 - 65536
+            collective_id=0, has_side_effects=True, vmem_limit_bytes=VMEM
         ),
         name="layer",
-    )(x, dy, gains, w_o, w_q, w_ab, w_d, rope)
+    )(x, dy, gain_a, gain_m, w_o, w_q, w_ab, w_d, rope)
+
+
+def settle_kernel(count, *refs):
+    ins, outs, held = refs[:count], refs[count : 2 * count + 1], refs[2 * count + 1 : 3 * count + 1]
+    load_sem, store_sem = refs[3 * count + 1 :]
+    loads = [pltpu.make_async_copy(a, b, load_sem.at[i]) for i, (a, b) in enumerate(zip(ins, held))]
+    for copy in loads:
+        copy.start()
+    sources = [[h] for h in held]
+    sources[2] = [held[2].at[pl.ds(0, 1), :], held[2].at[pl.ds(1, 1), :]]
+    stores = []
+    for copy, parts in zip(loads, sources):
+        copy.wait()
+        for part in parts:
+            store = pltpu.make_async_copy(part, outs[len(stores)], store_sem.at[len(stores)])
+            store.start()
+            stores.append(store)
+    for store in stores:
+        store.wait()
+
+
+def settle(out, gtok, g_n, *rest):
+    arrays = (out, gtok, g_n) + rest
+    row = jax.ShapeDtypeStruct((1, g_n.shape[1]), F32)
+    like = [jax.ShapeDtypeStruct(a.shape, a.dtype) for a in arrays]
+    shapes = (*like[:2], row, row, *like[3:])
+    hbm = pl.BlockSpec(memory_space=pl.ANY)
+    return pl.pallas_call(
+        functools.partial(settle_kernel, len(arrays)),
+        out_shape=shapes,
+        in_specs=[hbm] * len(arrays),
+        out_specs=(hbm,) * len(shapes),
+        scratch_shapes=[pltpu.VMEM(a.shape, a.dtype) for a in arrays]
+        + [pltpu.SemaphoreType.DMA((len(arrays),)), pltpu.SemaphoreType.DMA((len(shapes),))],
+        compiler_params=pltpu.CompilerParams(vmem_limit_bytes=VMEM),
+        name="settle",
+    )(*arrays)
 
 
 def rope_table():
@@ -846,16 +1113,24 @@
     x = turn(tokens, outer, LOW)
     dy = turn(grad_output, outer, LOW)
     p = Plan(nz, D, T, w_qkv.shape[2], w_in.shape[2])
-    U, L, H, heads, real = p.units, p.lane, p.hid, p.heads, p.real
-    gain_rows = jnp.pad(jnp.stack(gains), ((0, 14), (0, 0)))
-    qkv_rows = w_qkv.reshape(L, 3, 2, heads, HD).transpose(2, 3, 1, 4, 0).reshape(6 * U, L)
-    in_rows = jnp.pad(w_in.transpose(1, 2, 0), ((0, 0), (0, 2 * H - real), (0, 0)))
-    down_rows = jnp.pad(w_down, ((0, 2 * H - real), (0, 0)))
+    L = p.lane
     rope = jnp.asarray(rope_table())
-    out, gtok, g_n, g_out, g_q, g_ab, g_down = layer(p, x, dy, gain_rows, w_out, qkv_rows, in_rows, down_rows, rope)
+    results = layer(
+        p,
+        x,
+        dy,
+        gains[0].reshape(1, L),
+        gains[1].reshape(1, L),
+        w_out,
+        w_qkv.transpose(1, 0, 2),
+        w_in.transpose(1, 2, 0),
+        w_down,
+        rope,
+    )
+    out, gtok, g_a, g_m, g_out, g_q, g_ab, g_down = settle(*results)
 
     out, gtok = turn(out, LOW, outer), turn(gtok, LOW, outer)
-    g_qkv = g_q.reshape(2, heads, 3, HD, L).transpose(4, 2, 0, 1, 3).reshape(L, 3, 2 * U)
+    g_qkv = g_q.transpose(1, 0, 2)
     g_in = g_ab.transpose(2, 0, 1)
     return (
         out,
@@ -864,8 +1139,8 @@
         narrow(g_out, 1),
         narrow(g_in, 0),
         narrow(g_down, 1),
-        narrow(g_n[0], 0),
-        narrow(g_n[1], 0),
+        narrow(g_a.reshape(L), 0),
+        narrow(g_m.reshape(L), 0),
     )
 
 

time: 284 us -> 258 us (0.908)
  Pallas kernels: 270 us -> 257 us
  local copies, waits for them, and re-layouts: 12.6 us -> 0 us
    pallas_call x1, Pallas kernels: 270 us -> 254 us  [layer(): pl.pallas_call(functools.partial(kernel, p), out_shape=(jax.ShapeDtypeStr...]
    unnamed x25 -> x0, local copies, waits for them, and re-layouts: 8.15 us -> none
    pallas_call x0 -> x1, Pallas kernels: none -> 3.18 us  [settle(): pl.pallas_call(functools.partial(settle_kernel, len(arrays)), out_shape=s...]
where the time goes in v3:
time: 258 us
  Pallas kernels  257 us (100%)
    pallas_call x1, Pallas kernels, layer(): pl.pallas_call(functools.partial(kernel, p), out_shape=(jax.ShapeDtypeStr...  254 us

profile of v3, /device:TPU:0, one launch (start us, length us, event | category | flops | bytes accessed | tf_op | source)
XLA Modules:
  0.0 258.0 jit_solution(15767229773016628156)
XLA Ops:
  0.6 254.0 %layer.1 = (bf16[512,1024]{1,0:T(8,128)(2,1)}, bf16[512,1024]{1,0:T(8,128)(2,1)}, f32[16,128]{1,0:T(8,128)}, f32[256,128]{1,0:T(8,128)}, f32[3,128,256]{2,1,0:T(...) custom-call(bf16[512,1024]{1,0:T(8,128)(2,1)} %x_hbm.1, bf16[512,1024]{1,0:T(8,128)(2,1)} %dy_hbm.1, ...), custom_call_target="tpu_custom_call" | custom-call | tf_op jit(solution)/shard_map/layer/pallas_call | solution.py:1026
  254.6 3.2 %settle.1 = (bf16[512,1024]{1,0:T(8,128)(2,1)}, bf16[512,1024]{1,0:T(8,128)(2,1)}, f32[1,128]{1,0:T(1,128)}, f32[1,128]{1,0:T(1,128)}, f32[256,128]{1,0:T(8,128)...) custom-call(bf16[512,1024]{1,0:T(8,128)(2,1)} %get-tuple-element.23.refs_0_, ...), custom_call_target="tpu_custom_call" | custom-call | tf_op jit(solution)/shard_map/settle/pallas_call | solution.py:1072
